TPU v7x, 32 devices: a whole 2x2x4 slice. The times are simulated.
32 devices in a mesh: pipe: 2 (over x), tensor: 4 (over z), dp: 4 (over y, core).
Axes of the slice: x: 2, y: 2, z: 4, core: 2. Of those that a mesh axis runs over, the one named last changes fastest.
Arguments:
- section_layers: int32 [2], replicated, may hold values from 9 to 11
- grad_out: bfloat16 [2, 4, 192, 4096], P('pipe', 'dp', 'tensor'), may hold values from -6 to 6
- gate_act: bfloat16 [2, 4, 192, 28672], P('pipe', 'dp', None, 'tensor'), may hold values from -6 to 6
- up_act: bfloat16 [2, 4, 192, 28672], P('pipe', 'dp', None, 'tensor'), may hold values from -6 to 6
- down_weight: bfloat16 [2, 28672, 4096], P('pipe', 'tensor'), may hold values from -0.09375 to 0.09375
Outputs:
- grad_gate: bfloat16 [2, 4, 192, 28672], P('pipe', 'dp', None, 'tensor')
- grad_up: bfloat16 [2, 4, 192, 28672], P('pipe', 'dp', None, 'tensor')
- grad_down_w: bfloat16 [2, 28672, 4096], P('pipe', ('tensor', 'dp'))
All inputs are finite; a program needn't handle non-finite values.
Results may differ from a plain program's by a relative error of at most 0.013.
Values may be sent and summed in bfloat16 or wider, within the bound.
No kernel may reach another device: no remote copies, remote signals or barrier semaphores. Data moves between devices by JAX's collectives and lax.ppermute only.
A program may use at most 192 MiB of HBM per device.

v0:
```python
import jax
import jax.numpy as jnp
from jax import lax
from jax.sharding import PartitionSpec as P


def per_device(section_layers, grad_out, gate_act, up_act, down_weight):
    section = lax.axis_index("pipe")
    positions = jnp.arange(section_layers.shape[0], dtype=jnp.int32)
    offset = jnp.sum(jnp.where(positions < section, section_layers, 0))
    layers_here = jnp.sum(jnp.where(positions == section, section_layers, 0))
    scale = jnp.sqrt(10.0 / (offset + layers_here).astype(jnp.float32))
    gate = gate_act[0, 0].astype(jnp.float32)
    up = up_act[0, 0].astype(jnp.float32)
    logistic = jax.nn.sigmoid(gate)
    activated = gate * logistic
    hidden = (activated * up).astype(jnp.bfloat16)
    weight = down_weight[0]
    all_rows = lax.all_gather(grad_out[0, 0], "tensor", axis=0, tiled=True)
    grad_hidden = scale * lax.dot_general(
        all_rows, weight, (((1,), (1,)), ((), ())), preferred_element_type=jnp.float32
    )
    grad_gate = (grad_hidden * up * logistic * (1.0 + gate * (1.0 - logistic))).astype(jnp.bfloat16)
    grad_up = (grad_hidden * activated).astype(jnp.bfloat16)
    replicas = lax.axis_size("dp")
    norm_scale = scale / jnp.sqrt(jnp.float32(hidden.shape[0] * replicas))
    summed = lax.psum_scatter(
        (
            norm_scale
            * lax.dot_general(
                hidden, all_rows, (((0,), (0,)), ((), ())), preferred_element_type=jnp.float32
            )
        ).astype(jnp.bfloat16),
        "dp",
        scatter_dimension=0,
        tiled=True,
    )
    grad_down_w = summed[None]
    return (grad_gate[None, None], grad_up[None, None], grad_down_w)


def solution(mesh):
    placed = (
        P(),
        P("pipe", "dp", "tensor", None),
        P("pipe", "dp", None, "tensor"),
        P("pipe", "dp", None, "tensor"),
        P("pipe", "tensor", None),
    )
    return jax.shard_map(
        per_device,
        mesh=mesh,
        in_specs=placed,
        out_specs=(
            P("pipe", "dp", None, "tensor"),
            P("pipe", "dp", None, "tensor"),
            P("pipe", ("tensor", "dp"), None),
        ),
        check_vma=False,
    )
```

profile of v0, /device:TPU:0, one launch (start us, length us, event | category | flops | bytes accessed | tf_op | source)
XLA Modules:
  0.0 477.1 jit_solution(10743920367793809079)
XLA Ops:
  7.2 0.0 all-gather.3.cloned.1.call-start
  7.2 0.7 all-gather.3.cloned.1.call-update
  7.9 0.0 reduce-scatter.2.cloned.1.call-start
  7.9 1.3 fusion.20
  10.6 4.3 fusion.29
  15.0 34.4 %all-gather.3.cloned.1.call-done = bf16[1,1,192,4096]{3,2,1,0:T(8,128)(2,1)} async-done(((bf16[1,1,48,4096]{3,2,1,0:T(8,128)(2,1)}), bf16[1,1,192,4096]{3,2,1,0:T(8,128)(2,1)}) %all-gather.3.cloned.1.call-update) | async-done | bytes 1572880 | tf_op jit(solution)/shard_map/all_gather | solution.py:19
  49.4 24.2 %multiply_convert_fusion = bf16[7168,4096]{1,0:T(8,128)(2,1)} fusion(f32[]{:T(128)S(6)} %div.11, bf16[1,1,192,4096]{3,2,1,0:T(8,128)(2,1)} %all-gather.3.cloned.1.call-done, bf16[192,7168]{1,0:T(8,128)(2,1)S(1)} %fusion.29), kind=kOutput, calls=%fused_computation | convolution fusion | flops 11333009408 | bytes 63045636 | tf_op jit(solution)/shard_map/dot_general | solution.py:30
  73.6 0.0 copy-start
  73.6 0.0 reduce-scatter.2.cloned.1.call-update
  73.6 1.8 copy-done
  75.3 39.1 %fusion.13 = (bf16[1,1,192,7168]{3,2,1,0:T(8,128)(2,1)}, bf16[1,1,192,7168]{3,2,1,0:T(8,128)(2,1)}) fusion(bf16[1,1,192,7168]{3,2,1,0:T(8,128)(2,1)S(1)} %copy-done, bf16[1,1,192,7168]{3,2,1,0:T(8,128)(2,1)} %param.8, bf16[1,7168,4096]{2,1,0:T(8,128)(2,1)} %param.9, bf16[1,1,192,4096]{3,2,1,0:T(8,128)(2,1)} %all-gather.3.cloned.1.call-done, f32[]{:T(128)S(6)} %sqrt.3), kind=kOutput, calls=%fused_computation.18 | convolution fusion | flops 11296309248 | bytes 71303168 | tf_op jit(solution)/shard_map/dot_general | solution.py:20
  114.5 355.8 %reduce-scatter.2.cloned.1.call-done = bf16[1792,4096]{1,0:T(8,128)(2,1)} async-done(((bf16[7168,4096]{1,0:T(8,128)(2,1)}), bf16[1792,4096]{1,0:T(8,128)(2,1)}) %reduce-scatter.2.cloned.1.call-update) | async-done | bytes 14680080 | tf_op jit(solution)/shard_map/reduce_scatter | solution.py:27
Async XLA Ops:
  7.2 42.2 %all-gather.3.cloned.1.call-start = ((), (), s32[]{:S(2)}) async-start(), calls=%async_computation.2 | async-start | bytes 1966080 | tf_op jit(solution)/shard_map/all_gather | solution.py:19
  7.9 462.3 %reduce-scatter.2.cloned.1.call-start = ((), (), s32[]{:S(2)}) async-start(), calls=%async_computation.1 | async-start | bytes 73400320 | tf_op jit(solution)/shard_map/reduce_scatter | solution.py:27
  73.6 1.8 copy-start
Sparse Core Ops, SparseCore 0:
  9.6 39.7 all-gather.2
  73.7 396.4 reduce-scatter.1
where the time goes:
time: 477 us
  waiting for transfers between devices  391 us (82%)
  matrix products  63.3 us (13%)
  between operations  15.4 us (3%)
  other arithmetic  5.65 us (1%)
    reduce_scatter x1, waiting for transfers between devices, per_device(): lax.psum_scatter((norm_scale * lax.dot_general(hidden, all_rows, (((0,),...  356 us
    dot_general x1, matrix products, per_device(): lax.dot_general(all_rows, weight, (((1,), (1,)), ((), ())), preferred_ele...  39.1 us
    all_gather x1, waiting for transfers between devices, per_device(): all_rows = lax.all_gather(grad_out[0, 0], 'tensor', axis=0, tiled=True)  34.4 us
    dot_general x1, matrix products, per_device(): lax.dot_general(hidden, all_rows, (((0,), (0,)), ((), ())), preferred_ele...  24.2 us
  transfers between devices with their start and end apart: 2, of which 2 were waited for; matrix products, arithmetic and copies ran while one was open for 9% of the time, Pallas kernels for 0%

commit v1 on v0

v1 whole, which is shorter than its diff:
```python
import jax
import jax.numpy as jnp
from jax import lax
from jax.sharding import PartitionSpec as P


def section_scale(section_layers):
    section = lax.axis_index("pipe")
    positions = jnp.arange(section_layers.shape[0], dtype=jnp.int32)
    offset = jnp.sum(jnp.where(positions < section, section_layers, 0))
    layers_here = jnp.sum(jnp.where(positions == section, section_layers, 0))
    return jnp.sqrt(10.0 / (offset + layers_here).astype(jnp.float32))


def in_order(slots, place):
    count, rows = len(slots), slots[0].shape[0]
    whole = jnp.zeros((count * rows, slots[0].shape[1]), slots[0].dtype)
    for j, slot in enumerate(slots):
        block = lax.rem(place - j + count, count)
        whole = lax.dynamic_update_slice(whole, slot, (block * rows, 0))
    return whole


def per_device(section_layers, grad_out, gate_act, up_act, down_weight):
    scale = section_scale(section_layers)
    tensor, replicas = lax.axis_size("tensor"), lax.axis_size("dp")
    place, replica = lax.axis_index("tensor"), lax.axis_index("dp")
    own_rows = grad_out[0, 0]
    weight = down_weight[0]
    ring = [(i, (i + 1) % tensor) for i in range(tensor)]
    pair = [(i, i ^ 1) for i in range(replicas)]
    half = replicas // 2

    gate = gate_act[0, 0].astype(jnp.float32)
    up = up_act[0, 0].astype(jnp.float32)
    logistic = jax.nn.sigmoid(gate)
    activated = gate * logistic
    hidden = (activated * up).astype(jnp.bfloat16)
    rows, width = hidden.shape
    block = width // replicas

    def columns_of(owner, count=1):
        return lax.dynamic_slice(hidden, (0, owner * block), (rows, block * count))

    own_chip = replica // 2 * 2
    core = replica - own_chip
    row_parts, hidden_parts = [own_rows], []
    sent_hidden = []
    for step in range(1, half):
        to = [(i, (i + 2 * step) % replicas) for i in range(replicas)]
        row_parts.append(lax.ppermute(own_rows, "dp", to))
        sent_hidden.append(
            lax.ppermute(columns_of((own_chip + 2 * step) % replicas, 2), "dp", to)
        )
    mine, others = [columns_of(replica)], [columns_of(own_chip + 1 - core)]
    for pieces in sent_hidden:
        mine.append(lax.dynamic_slice(pieces, (0, core * block), (rows, block)))
        others.append(lax.dynamic_slice(pieces, (0, (1 - core) * block), (rows, block)))
    crossed = [lax.ppermute(piece, "dp", pair) for piece in others]

    gathered = []
    for part in row_parts:
        slots = [part]
        for _ in range(tensor - 1):
            slots.append(lax.ppermute(slots[-1], "tensor", ring))
        gathered.append(in_order(slots, place))
    all_rows = gathered[0]
    crossed_rows = [lax.ppermute(part, "dp", pair) for part in gathered]

    grad_hidden = scale * lax.dot_general(
        all_rows, weight, (((1,), (1,)), ((), ())), preferred_element_type=jnp.float32
    )
    grad_gate = (grad_hidden * up * logistic * (1.0 + gate * (1.0 - logistic))).astype(jnp.bfloat16)
    grad_up = (grad_hidden * activated).astype(jnp.bfloat16)

    norm_scale = scale / jnp.sqrt(jnp.float32(rows * replicas))
    every_hidden = jnp.concatenate(mine + crossed, axis=0)
    every_row = jnp.concatenate(gathered + crossed_rows, axis=0)
    summed = norm_scale * lax.dot_general(
        every_hidden, every_row, (((0,), (0,)), ((), ())), preferred_element_type=jnp.float32
    )
    grad_down_w = summed.astype(jnp.bfloat16)[None]
    return (grad_gate[None, None], grad_up[None, None], grad_down_w)


def solution(mesh):
    placed = (
        P(),
        P("pipe", "dp", "tensor", None),
        P("pipe", "dp", None, "tensor"),
        P("pipe", "dp", None, "tensor"),
        P("pipe", "tensor", None),
    )
    return jax.shard_map(
        per_device,
        mesh=mesh,
        in_specs=placed,
        out_specs=(
            P("pipe", "dp", None, "tensor"),
            P("pipe", "dp", None, "tensor"),
            P("pipe", ("tensor", "dp"), None),
        ),
        check_vma=False,
    )
```

time: 477 us -> 132 us (0.28)
  waiting for transfers between devices: 391 us -> 59.3 us
  matrix products: 63.3 us -> 47.2 us
  between operations: 15.4 us -> 2.09 us
  local copies, waits for them, and re-layouts: 1.75 us -> 13.5 us
  starting transfers between devices: 0.08 us -> 7.99 us
    reduce_scatter x1 -> x0, waiting for transfers between devices: 356 us -> none  [per_device(): lax.psum_scatter((norm_scale * lax.dot_general(hidden, all_rows, (((0,),...]
    ppermute x0 -> x12, waiting for transfers between devices: none -> 59.3 us  [the longest x6 41.2 us: per_device(): slots.append(lax.ppermute(slots[-1], 'tensor', ring))]
    all_gather x1 -> x0, waiting for transfers between devices: 34.4 us -> none  [per_device(): all_rows = lax.all_gather(grad_out[0, 0], 'tensor', axis=0, tiled=True)]
    dot_general x1, matrix products: 39.1 us -> 30.5 us  [per_device(): lax.dot_general(all_rows, weight, (((1,), (1,)), ((), ())), preferred_ele...]
    ppermute x0 -> x12, starting transfers between devices: none -> 7.99 us  [the longest x6 4.37 us: per_device(): slots.append(lax.ppermute(slots[-1], 'tensor', ring))]
    dot_general x1, matrix products: 24.2 us -> 16.8 us  [per_device(): lax.dot_general(every_hidden, every_row, (((0,), (0,)), ((), ())), prefer...]
    dynamic_update_slice x0 -> x8, local copies, waits for them, and re-layouts: none -> 7.26 us  [in_order(): whole = lax.dynamic_update_slice(whole, slot, (block * rows, 0))]
  transfers between devices with their start and end apart: 2 -> 12, of which waited for: 2 -> 7; matrix products, arithmetic and copies ran while one was open for 9% -> 34% of each run, Pallas kernels for 0% -> 0%
where the time goes in v1:
time: 132 us; the launch traced here: 131 us
  waiting for transfers between devices  59.3 us (45%)
  matrix products  47.2 us (36%)
  local copies, waits for them, and re-layouts  13.5 us (10%)
  starting transfers between devices  7.99 us (6%)
  between operations  2.09 us (2%)
    ppermute x6, waiting for transfers between devices, per_device(): slots.append(lax.ppermute(slots[-1], 'tensor', ring))  41.2 us
    dot_general x1, matrix products, per_device(): lax.dot_general(all_rows, weight, (((1,), (1,)), ((), ())), preferred_ele...  30.5 us
    dot_general x1, matrix products, per_device(): lax.dot_general(every_hidden, every_row, (((0,), (0,)), ((), ())), prefer...  16.8 us
    ppermute x1, waiting for transfers between devices, per_device(): lax.ppermute(columns_of((own_chip + 2 * step) % replicas, 2), 'dp', to)  16 us
    dynamic_update_slice x8, local copies, waits for them, and re-layouts, in_order(): whole = lax.dynamic_update_slice(whole, slot, (block * rows, 0))  7.26 us
    ppermute x6, starting transfers between devices, per_device(): slots.append(lax.ppermute(slots[-1], 'tensor', ring))  4.37 us
    another operation x2, local copies, waits for them, and re-layouts  2.67 us
  transfers between devices with their start and end apart: 12, of which 7 were waited for; matrix products, arithmetic and copies ran while one was open for 34% of the time, Pallas kernels for 0%

profile of v1, /device:TPU:0, one launch (start us, length us, event | category | flops | bytes accessed | tf_op | source)
XLA Modules:
  0.0 131.5 jit_solution(1585565945144410871)
XLA Ops:
  0.6 3.1 %collective-permute-start = (bf16[48,4096]{1,0:T(8,128)(2,1)}, bf16[48,4096]{1,0:T(8,128)(2,1)S(1)}, u32[]{:S(2)}, u32[]{:S(2)}) collective-permute-start(bf16[48,4096]{1,0:T(8,128)(2,1)} %bitcast.32), channel_id=1, source_target_pairs={{0,4},{4,8},{8,12},{12,0},{1,5},{5,9},{9,13},{13,1},{2,6},{6,10},{... | collective-permute-start | bytes 1179656 | tf_op jit(solution)/shard_map/ppermute | solution.py:65
  3.7 1.5 %collective-permute-start.6 = (bf16[48,4096]{1,0:T(8,128)(2,1)}, bf16[48,4096]{1,0:T(8,128)(2,1)S(1)}, u32[]{:S(2)}, u32[]{:S(2)}) collective-permute-start(bf16[48,4096]{1,0:T(8,128)(2,1)} %bitcast.33), channel_id=1, source_target_pairs={{0,2},{1,3},{2,0},{3,1},{4,6},{5,7},{6,4},{7,5},{8,10},{9,11},{10,... | collective-permute-start | bytes 1179656 | tf_op jit(solution)/shard_map/ppermute | solution.py:51
  5.2 1.3 %broadcast.12.clone = bf16[192,4096]{1,0:T(8,128)(2,1)} broadcast(bf16[]{:T(256)} %constant.61.clone.1), dimensions={} | broadcast | bytes 1572866 | tf_op jit(solution)/shard_map/broadcast.2
  6.6 1.8 %constant_dynamic-update-slice_fusion.7 = bf16[192,4096]{1,0:T(8,128)(2,1)} fusion(bf16[192,4096]{1,0:T(8,128)(2,1)} %broadcast.12.clone, s32[]{:T(128)S(6)} %select_n.51, bf16[1,1,48,4096]{3,2,1,0:T(8,128)(2,1)} %param.6), kind=kLoop, calls=%fused_computation.47 | loop fusion | bytes 786436 | tf_op jit(solution)/shard_map/dynamic_update_slice | solution.py:20
  8.3 1.3 fusion.31
  11.0 4.0 %collective-permute-done = bf16[48,4096]{1,0:T(8,128)(2,1)S(1)} collective-permute-done((bf16[48,4096]{1,0:T(8,128)(2,1)}, bf16[48,4096]{1,0:T(8,128)(2,1)S(1)}, u32[]{:S(2)}, u32[]{:S(2)}) %collective-permute-start) | collective-permute-done | bytes 393248 | tf_op jit(solution)/shard_map/ppermute | solution.py:65
  15.1 0.0 collective-permute-start.1
  15.1 0.0 collective-permute-done.6
  15.1 1.3 collective-permute-start.7
  16.4 1.3 %broadcast.12.clone.1 = bf16[192,4096]{1,0:T(8,128)(2,1)} broadcast(bf16[]{:T(256)} %constant.61.clone.1), dimensions={} | broadcast | bytes 1572866 | tf_op jit(solution)/shard_map/broadcast.2
  17.7 0.8 constant_dynamic-update-slice_fusion.3
  18.5 0.8 constant_dynamic-update-slice_fusion.6
  19.3 9.6 %collective-permute-done.1 = bf16[48,4096]{1,0:T(8,128)(2,1)S(1)} collective-permute-done((bf16[48,4096]{1,0:T(8,128)(2,1)S(1)}, bf16[48,4096]{1,0:T(8,128)(2,1)S(1)}, u32[]{:S(2)}, u32[]{:S(2)}) %collective-permute-start.1) | collective-permute-done | bytes 393248 | tf_op jit(solution)/shard_map/ppermute | solution.py:65
  28.9 0.0 collective-permute-start.2
  28.9 8.4 %collective-permute-done.7 = bf16[48,4096]{1,0:T(8,128)(2,1)S(1)} collective-permute-done((bf16[48,4096]{1,0:T(8,128)(2,1)S(1)}, bf16[48,4096]{1,0:T(8,128)(2,1)S(1)}, u32[]{:S(2)}, u32[]{:S(2)}) %collective-permute-start.7) | collective-permute-done | bytes 393248 | tf_op jit(solution)/shard_map/ppermute | solution.py:65
  37.3 0.0 collective-permute-start.8
  37.3 0.8 constant_dynamic-update-slice_fusion.2
  38.1 0.8 constant_dynamic-update-slice_fusion.5
  38.9 6.9 %collective-permute-done.2 = bf16[48,4096]{1,0:T(8,128)(2,1)S(1)} collective-permute-done((bf16[48,4096]{1,0:T(8,128)(2,1)S(1)}, bf16[48,4096]{1,0:T(8,128)(2,1)S(1)}, u32[]{:S(2)}, u32[]{:S(2)}) %collective-permute-start.2) | collective-permute-done | bytes 393248 | tf_op jit(solution)/shard_map/ppermute | solution.py:65
  45.8 0.8 constant_dynamic-update-slice_fusion.4
  46.5 0.0 collective-permute-start.10
  46.6 30.5 %fusion.21 = (bf16[1,1,192,7168]{3,2,1,0:T(8,128)(2,1)}, bf16[1,1,192,7168]{3,2,1,0:T(8,128)(2,1)}, bf16[192,7168]{1,0:T(8,128)(2,1)S(1)}) fusion(bf16[1,1,192,7168]{3,2,1,0:T(8,128)(2,1)} %param.7, bf16[1,1,192,7168]{3,2,1,0:T(8,128)(2,1)} %param.8, bf16[192,4096]{1,0:T(8,128)(2,1)} %constant_dynamic-update-slice_fusion.4, ...), kind=kOutput, calls=%fused_computation.26 | convolution fusion | flops 11299061760 | bytes 74055680 | tf_op jit(solution)/shard_map/dot_general | solution.py:70
  77.0 1.2 constant_dynamic-slice_fusion.3
  78.2 1.5 %collective-permute-start.3 = (bf16[192,3584]{1,0:T(8,128)(2,1)}, bf16[192,3584]{1,0:T(8,128)(2,1)}, u32[]{:S(2)}, u32[]{:S(2)}) collective-permute-start(bf16[192,3584]{1,0:T(8,128)(2,1)} %constant_dynamic-slice_fusion.3), channel_id=1, source_target_pairs={{0,2},{1,3},{2,0},{3,1},{4,6},{5,7},{6,4},{7,5},{8,10},{9,11},{10,... | collective-permute-start | bytes 4128776 | tf_op jit(solution)/shard_map/ppermute | solution.py:53
  79.7 0.0 collective-permute-done.8
  79.7 0.0 collective-permute-start.9
  79.7 0.8 constant_dynamic-update-slice_fusion.1
  80.5 12.2 %collective-permute-done.9 = bf16[48,4096]{1,0:T(8,128)(2,1)S(1)} collective-permute-done((bf16[48,4096]{1,0:T(8,128)(2,1)S(1)}, bf16[48,4096]{1,0:T(8,128)(2,1)S(1)}, u32[]{:S(2)}, u32[]{:S(2)}) %collective-permute-start.9) | collective-permute-done | bytes 393248 | tf_op jit(solution)/shard_map/ppermute | solution.py:65
  92.7 0.8 constant_dynamic-update-slice_fusion
  93.5 0.0 collective-permute-start.11
  93.5 1.0 constant_dynamic-slice_fusion.4
  94.5 0.5 collective-permute-start.4
  95.0 16.0 %collective-permute-done.3 = bf16[192,3584]{1,0:T(8,128)(2,1)} collective-permute-done((bf16[192,3584]{1,0:T(8,128)(2,1)}, bf16[192,3584]{1,0:T(8,128)(2,1)}, u32[]{:S(2)}, u32[]{:S(2)}) %collective-permute-start.3) | collective-permute-done | bytes 1376288 | tf_op jit(solution)/shard_map/ppermute | solution.py:53
  111.1 1.4 %constant_dynamic-slice_fusion.2 = (bf16[192,1792]{1,0:T(8,128)(2,1)S(1)}, bf16[192,1792]{1,0:T(8,128)(2,1)S(1)}) fusion(bf16[192,3584]{1,0:T(8,128)(2,1)} %collective-permute-done.3, s32[]{:T(128)S(6)} %select_n.59, s32[]{:T(128)S(6)} %select_n.61), kind=kLoop, calls=%fused_computation.41 | loop fusion | bytes 2752520 | tf_op jit(solution)/shard_map/dynamic_slice | solution.py:57
  112.5 0.1 collective-permute-start.5
  112.5 0.0 collective-permute-done.4
  112.6 0.0 collective-permute-done.10
  112.6 0.0 collective-permute-done.11
  112.6 2.1 %collective-permute-done.5 = bf16[192,1792]{1,0:T(8,128)(2,1)S(1)} collective-permute-done((bf16[192,1792]{1,0:T(8,128)(2,1)S(1)}, bf16[192,1792]{1,0:T(8,128)(2,1)S(1)}, u32[]{:S(2)}, u32[]{:S(2)}) %collective-permute-start.5) | collective-permute-done | bytes 688160 | tf_op jit(solution)/shard_map/ppermute | solution.py:59
  114.7 16.8 %fusion.2 = bf16[1,1792,4096]{2,1,0:T(8,128)(2,1)} fusion(f32[]{:T(128)S(6)} %div.19, bf16[192,4096]{1,0:T(8,128)(2,1)} %collective-permute-done.11, bf16[192,4096]{1,0:T(8,128)(2,1)} %collective-permute-done.10, bf16[192,4096]{1,0:T(8,128)(2,1)} %constant_dynamic-update-slice_fusion, bf16[192,4096]{1,0:T(8,128)(2,1)} %constant_dynamic-update-slice_fusion.4, ...), kind=kOutput, calls=%fused_computation.3 | convolution fusion | flops 11325145088 | bytes 23724036 | tf_op jit(solution)/shard_map/dot_general | solution.py:79
Async XLA Ops:
  0.6 14.4 %collective-permute-start = (bf16[48,4096]{1,0:T(8,128)(2,1)}, bf16[48,4096]{1,0:T(8,128)(2,1)S(1)}, u32[]{:S(2)}, u32[]{:S(2)}) collective-permute-start(bf16[48,4096]{1,0:T(8,128)(2,1)} %bitcast.32), channel_id=1, source_target_pairs={{0,4},{4,8},{8,12},{12,0},{1,5},{5,9},{9,13},{13,1},{2,6},{6,10},{... | collective-permute-start | bytes 1179656 | tf_op jit(solution)/shard_map/ppermute | solution.py:65
  3.7 11.4 %collective-permute-start.6 = (bf16[48,4096]{1,0:T(8,128)(2,1)}, bf16[48,4096]{1,0:T(8,128)(2,1)S(1)}, u32[]{:S(2)}, u32[]{:S(2)}) collective-permute-start(bf16[48,4096]{1,0:T(8,128)(2,1)} %bitcast.33), channel_id=1, source_target_pairs={{0,2},{1,3},{2,0},{3,1},{4,6},{5,7},{6,4},{7,5},{8,10},{9,11},{10,... | collective-permute-start | bytes 1179656 | tf_op jit(solution)/shard_map/ppermute | solution.py:51
  15.1 13.8 %collective-permute-start.1 = (bf16[48,4096]{1,0:T(8,128)(2,1)S(1)}, bf16[48,4096]{1,0:T(8,128)(2,1)S(1)}, u32[]{:S(2)}, u32[]{:S(2)}) collective-permute-start(bf16[48,4096]{1,0:T(8,128)(2,1)S(1)} %collective-permute-done), channel_id=1, source_target_pairs={{0,4},{4,8},{8,12},{12,0},{1,5},{5,9},{9,13},{13,1},{2,6},{6,10},{... | collective-permute-start | bytes 1179656 | tf_op jit(solution)/shard_map/ppermute | solution.py:65
  15.1 22.3 %collective-permute-start.7 = (bf16[48,4096]{1,0:T(8,128)(2,1)S(1)}, bf16[48,4096]{1,0:T(8,128)(2,1)S(1)}, u32[]{:S(2)}, u32[]{:S(2)}) collective-permute-start(bf16[48,4096]{1,0:T(8,128)(2,1)S(1)} %collective-permute-done.6), channel_id=1, source_target_pairs={{0,4},{4,8},{8,12},{12,0},{1,5},{5,9},{9,13},{13,1},{2,6},{6,10},{... | collective-permute-start | bytes 1179656 | tf_op jit(solution)/shard_map/ppermute | solution.py:65
  28.9 16.9 %collective-permute-start.2 = (bf16[48,4096]{1,0:T(8,128)(2,1)S(1)}, bf16[48,4096]{1,0:T(8,128)(2,1)S(1)}, u32[]{:S(2)}, u32[]{:S(2)}) collective-permute-start(bf16[48,4096]{1,0:T(8,128)(2,1)S(1)} %collective-permute-done.1), channel_id=1, source_target_pairs={{0,4},{4,8},{8,12},{12,0},{1,5},{5,9},{9,13},{13,1},{2,6},{6,10},{... | collective-permute-start | bytes 1179656 | tf_op jit(solution)/shard_map/ppermute | solution.py:65
  37.3 42.4 %collective-permute-start.8 = (bf16[48,4096]{1,0:T(8,128)(2,1)S(1)}, bf16[48,4096]{1,0:T(8,128)(2,1)S(1)}, u32[]{:S(2)}, u32[]{:S(2)}) collective-permute-start(bf16[48,4096]{1,0:T(8,128)(2,1)S(1)} %collective-permute-done.7), channel_id=1, source_target_pairs={{0,4},{4,8},{8,12},{12,0},{1,5},{5,9},{9,13},{13,1},{2,6},{6,10},{... | collective-permute-start | bytes 1179656 | tf_op jit(solution)/shard_map/ppermute | solution.py:65
  46.5 66.0 %collective-permute-start.10 = (bf16[192,4096]{1,0:T(8,128)(2,1)}, bf16[192,4096]{1,0:T(8,128)(2,1)}, u32[]{:S(2)}, u32[]{:S(2)}) collective-permute-start(bf16[192,4096]{1,0:T(8,128)(2,1)} %constant_dynamic-update-slice_fusion.4), channel_id=1, source_target_pairs={{0,1},{1,0},{2,3},{3,2},{4,5},{5,4},{6,7},{7,6},{8,9},{9,8},{10,11... | collective-permute-start | bytes 4718600 | tf_op jit(solution)/shard_map/ppermute | solution.py:68
  78.2 32.9 %collective-permute-start.3 = (bf16[192,3584]{1,0:T(8,128)(2,1)}, bf16[192,3584]{1,0:T(8,128)(2,1)}, u32[]{:S(2)}, u32[]{:S(2)}) collective-permute-start(bf16[192,3584]{1,0:T(8,128)(2,1)} %constant_dynamic-slice_fusion.3), channel_id=1, source_target_pairs={{0,2},{1,3},{2,0},{3,1},{4,6},{5,7},{6,4},{7,5},{8,10},{9,11},{10,... | collective-permute-start | bytes 4128776 | tf_op jit(solution)/shard_map/ppermute | solution.py:53
  79.7 13.0 %collective-permute-start.9 = (bf16[48,4096]{1,0:T(8,128)(2,1)S(1)}, bf16[48,4096]{1,0:T(8,128)(2,1)S(1)}, u32[]{:S(2)}, u32[]{:S(2)}) collective-permute-start(bf16[48,4096]{1,0:T(8,128)(2,1)S(1)} %collective-permute-done.8), channel_id=1, source_target_pairs={{0,4},{4,8},{8,12},{12,0},{1,5},{5,9},{9,13},{13,1},{2,6},{6,10},{... | collective-permute-start | bytes 1179656 | tf_op jit(solution)/shard_map/ppermute | solution.py:65
  93.5 19.1 %collective-permute-start.11 = (bf16[192,4096]{1,0:T(8,128)(2,1)}, bf16[192,4096]{1,0:T(8,128)(2,1)}, u32[]{:S(2)}, u32[]{:S(2)}) collective-permute-start(bf16[192,4096]{1,0:T(8,128)(2,1)} %constant_dynamic-update-slice_fusion), channel_id=1, source_target_pairs={{0,1},{1,0},{2,3},{3,2},{4,5},{5,4},{6,7},{7,6},{8,9},{9,8},{10,11... | collective-permute-start | bytes 4718600 | tf_op jit(solution)/shard_map/ppermute | solution.py:68
  94.5 18.0 %collective-permute-start.4 = (bf16[192,1792]{1,0:T(8,128)(2,1)}, bf16[192,1792]{1,0:T(8,128)(2,1)S(1)}, u32[]{:S(2)}, u32[]{:S(2)}) collective-permute-start(bf16[192,1792]{1,0:T(8,128)(2,1)} %get-tuple-element.9), channel_id=1, source_target_pairs={{0,1},{1,0},{2,3},{3,2},{4,5},{5,4},{6,7},{7,6},{8,9},{9,8},{10,11... | collective-permute-start | bytes 2064392 | tf_op jit(solution)/shard_map/ppermute | solution.py:59
  112.5 2.2 %collective-permute-start.5 = (bf16[192,1792]{1,0:T(8,128)(2,1)S(1)}, bf16[192,1792]{1,0:T(8,128)(2,1)S(1)}, u32[]{:S(2)}, u32[]{:S(2)}) collective-permute-start(bf16[192,1792]{1,0:T(8,128)(2,1)S(1)} %get-tuple-element.11), channel_id=1, source_target_pairs={{0,1},{1,0},{2,3},{3,2},{4,5},{5,4},{6,7},{7,6},{8,9},{9,8},{10,11... | collective-permute-start | bytes 2064392 | tf_op jit(solution)/shard_map/ppermute | solution.py:59

commit v2 on v1

--- a/solution.py
+++ b/solution.py
@@ -1,7 +1,15 @@
+import functools
+
 import jax
 import jax.numpy as jnp
 from jax import lax
+from jax.experimental import pallas as pl
+from jax.experimental.pallas import tpu as pltpu
 from jax.sharding import PartitionSpec as P
+
+VMEM_BYTES = 56 * 1024 * 1024
+UNIT_STEP = 256
+OUT_STEP = 512
 
 
 def section_scale(section_layers):
@@ -10,6 +18,10 @@
     offset = jnp.sum(jnp.where(positions < section, section_layers, 0))
     layers_here = jnp.sum(jnp.where(positions == section, section_layers, 0))
     return jnp.sqrt(10.0 / (offset + layers_here).astype(jnp.float32))
+
+
+def after(value, *earlier):
+    return lax.optimization_barrier((value, *earlier))[0]
 
 
 def in_order(slots, place):
@@ -21,7 +33,7 @@
     return whole
 
 
-def per_device(section_layers, grad_out, gate_act, up_act, down_weight):
+def general(section_layers, grad_out, gate_act, up_act, down_weight):
     scale = section_scale(section_layers)
     tensor, replicas = lax.axis_size("tensor"), lax.axis_size("dp")
     place, replica = lax.axis_index("tensor"), lax.axis_index("dp")
@@ -44,8 +56,7 @@
 
     own_chip = replica // 2 * 2
     core = replica - own_chip
-    row_parts, hidden_parts = [own_rows], []
-    sent_hidden = []
+    row_parts, sent_hidden = [own_rows], []
     for step in range(1, half):
         to = [(i, (i + 2 * step) % replicas) for i in range(replicas)]
         row_parts.append(lax.ppermute(own_rows, "dp", to))
@@ -79,11 +90,362 @@
     summed = norm_scale * lax.dot_general(
         every_hidden, every_row, (((0,), (0,)), ((), ())), preferred_element_type=jnp.float32
     )
-    grad_down_w = summed.astype(jnp.bfloat16)[None]
-    return (grad_gate[None, None], grad_up[None, None], grad_down_w)
+    return (grad_gate[None, None], grad_up[None, None], summed.astype(jnp.bfloat16)[None])
+
+
+def factors_kernel(at, gate, up, hidden, gate_factor, up_factor):
+    g, u = gate[...].astype(jnp.float32), up[...].astype(jnp.float32)
+    logistic = 0.5 + 0.5 * jnp.tanh(0.5 * g)
+    activated = g * logistic
+    slope = logistic + activated * (1.0 - logistic)
+    hidden[...] = (activated * u).astype(jnp.bfloat16)
+    gate_factor[...] = (u * slope).astype(jnp.bfloat16)
+    up_factor[...] = activated.astype(jnp.bfloat16)
+
+
+def factors(at, gate, up, block, first):
+    rows = gate.shape[0]
+    half = block // 2
+    out = jax.ShapeDtypeStruct((rows, block), jnp.bfloat16)
+    spec = pl.BlockSpec(
+        (rows, half), lambda i, at: (0, 2 * (at[first] if first >= 0 else -first - 1) + i)
+    )
+    return pl.pallas_call(
+        factors_kernel,
+        grid_spec=pltpu.PrefetchScalarGridSpec(
+            num_scalar_prefetch=1,
+            grid=(2,),
+            in_specs=[spec, spec],
+            out_specs=[pl.BlockSpec((rows, half), lambda i, at: (0, i))] * 3,
+        ),
+        out_shape=[out] * 3,
+        compiler_params=pltpu.CompilerParams(vmem_limit_bytes=VMEM_BYTES),
+        cost_estimate=pl.CostEstimate(flops=1000, bytes_accessed=1000, transcendentals=0),
+        name="factors",
+    )(at, gate, up)
+
+
+def assemble_kernel(at, *refs):
+    slots, whole = refs[:3], refs[3]
+    piece, width = slots[0].shape[0], whole.shape[1]
+    for j, slot in enumerate(slots):
+        block = lax.rem(at[2] - j + 4, 4)
+        there = pl.ds(pl.multiple_of(block * piece, piece), piece)
+        whole[there, :] = slot[:, :width]
+
+
+def assemble(at, slots, width):
+    piece = slots[0].shape[0]
+    return pl.pallas_call(
+        assemble_kernel,
+        grid_spec=pltpu.PrefetchScalarGridSpec(
+            num_scalar_prefetch=1,
+            grid=(1,),
+            in_specs=[pl.BlockSpec((piece, width), lambda i, at: (0, 0))] * 3,
+            out_specs=pl.BlockSpec((4 * piece, width), lambda i, at: (0, 0)),
+        ),
+        out_shape=jax.ShapeDtypeStruct((4 * piece, width), jnp.bfloat16),
+        compiler_params=pltpu.CompilerParams(vmem_limit_bytes=VMEM_BYTES),
+        cost_estimate=pl.CostEstimate(flops=1000, bytes_accessed=1000, transcendentals=0),
+        name="assemble",
+    )(at, *slots)
+
+
+def complete_kernel(at, slot, earlier, whole):
+    whole[...] = slot[...]
+
+
+def complete(at, slot, whole):
+    piece, width = slot.shape[0], whole.shape[1]
+    return pl.pallas_call(
+        complete_kernel,
+        grid_spec=pltpu.PrefetchScalarGridSpec(
+            num_scalar_prefetch=1,
+            grid=(1,),
+            in_specs=[
+                pl.BlockSpec((piece, width), lambda i, at: (0, 0)),
+                pl.BlockSpec(memory_space=pl.ANY),
+            ],
+            out_specs=pl.BlockSpec((piece, width), lambda i, at: (lax.rem(at[2] + 1, 4), 0)),
+        ),
+        out_shape=jax.ShapeDtypeStruct(whole.shape, jnp.bfloat16),
+        input_output_aliases={2: 0},
+        compiler_params=pltpu.CompilerParams(vmem_limit_bytes=VMEM_BYTES),
+        cost_estimate=pl.CostEstimate(flops=1000, bytes_accessed=1000, transcendentals=0),
+        name="complete",
+    )(at, slot, whole)
+
+
+def share_kernel(at, gate, up, gate_out, up_out):
+    gate_out[...] = gate[...]
+    up_out[...] = up[...]
+
+
+def share(at, gate, up, block, first):
+    rows = gate.shape[0]
+    out = jax.ShapeDtypeStruct((rows, 2 * block), jnp.bfloat16)
+    spec = pl.BlockSpec((rows, block), lambda i, at: (0, at[first + i]))
+    return pl.pallas_call(
+        share_kernel,
+        grid_spec=pltpu.PrefetchScalarGridSpec(
+            num_scalar_prefetch=1,
+            grid=(2,),
+            in_specs=[spec, spec],
+            out_specs=[pl.BlockSpec((rows, block), lambda i, at: (0, i))] * 2,
+        ),
+        out_shape=[out] * 2,
+        compiler_params=pltpu.CompilerParams(vmem_limit_bytes=VMEM_BYTES),
+        cost_estimate=pl.CostEstimate(flops=1000, bytes_accessed=1000, transcendentals=0),
+        name="share",
+    )(at, gate, up)
+
+
+def hidden_grad_kernel(at, scale, *refs):
+    slots, weight = refs[:8], refs[8]
+    own_mine, own_theirs, pair_mine, pair_theirs = refs[9:11], refs[11:13], refs[13:15], refs[15:17]
+    own_out, pair_out = refs[17:19], refs[19:21]
+    rows, product = refs[21:]
+    chip, place = at[1], at[2]
+    piece = slots[0].shape[0]
+    count = 4 * piece
+
+    @pl.when(pl.program_id(0) == 0)
+    def _():
+        for j in range(4):
+            block = lax.rem(place - j + 4, 4)
+            rows[pl.ds(pl.multiple_of(block * piece, piece), piece), :] = slots[j][...]
+            there = pl.ds(pl.multiple_of(count + block * piece, piece), piece)
+            rows[there, :] = slots[4 + j][...]
+
+    units = weight.shape[2]
+    both = weight[...].reshape(2 * units, weight.shape[3])
+    part = lax.dot_general(
+        rows[...], both, (((1,), (1,)), ((), ())), preferred_element_type=jnp.float32
+    )
+    product[0] = part[:, :units] * scale[0]
+    product[1] = part[:, units:] * scale[0]
+    for half, (own, pair) in enumerate(((own_mine, pair_mine), (own_theirs, pair_theirs))):
+        here = product[chip if half == 0 else 1 - chip]
+        for out, factor in zip(own_out, own):
+            out[half] = (here[:count] * factor[...].astype(jnp.float32)).astype(jnp.bfloat16)
+        for out, factor in zip(pair_out, pair):
+            out[half] = (here[count:] * factor[...].astype(jnp.float32)).astype(jnp.bfloat16)
+
+
+def hidden_grad(at, scale, slots, weight, factor_pairs, first, width):
+    rows, block = factor_pairs[0][0].shape
+    start = first // UNIT_STEP
+    depth = weight.shape[1]
+    halves = weight.reshape(2, 2, block, depth)
+    factor_args = [value for pair in factor_pairs for value in pair]
+    out = jax.ShapeDtypeStruct((2, rows, width), jnp.bfloat16)
+    return pl.pallas_call(
+        hidden_grad_kernel,
+        grid_spec=pltpu.PrefetchScalarGridSpec(
+            num_scalar_prefetch=1,
+            grid=(width // UNIT_STEP,),
+            in_specs=[pl.BlockSpec(memory_space=pltpu.SMEM)]
+            + [pl.BlockSpec(slot.shape, lambda i, at: (0, 0)) for slot in slots]
+            + [pl.BlockSpec((2, 1, UNIT_STEP, depth), lambda i, at: (0, at[0], start + i, 0))]
+            + [pl.BlockSpec((rows, UNIT_STEP), lambda i, at: (0, start + i))] * 8,
+            out_specs=[pl.BlockSpec((2, rows, UNIT_STEP), lambda i, at: (0, 0, i))] * 4
+            + [pl.BlockSpec((2 * rows, depth), lambda i, at: (0, 0))],
+            scratch_shapes=[pltpu.VMEM((2, 2 * rows, UNIT_STEP), jnp.float32)],
+        ),
+        out_shape=[out] * 4 + [jax.ShapeDtypeStruct((2 * rows, depth), jnp.bfloat16)],
+        compiler_params=pltpu.CompilerParams(vmem_limit_bytes=VMEM_BYTES),
+        cost_estimate=pl.CostEstimate(
+            flops=1000,
+            bytes_accessed=1000,
+            transcendentals=0,
+        ),
+        name="hidden_grad",
+    )(at, scale, *slots, halves, *factor_args)
+
+
+def weight_grad_kernel(low_steps, at, norm, *refs):
+    hidden, near, low, high = refs[:4], refs[4:6], refs[6:8], refs[8:16]
+    own_new, wholes, out, held, every = refs[16:18], refs[18:20], refs[20], refs[21], refs[22]
+    step = pl.program_id(0)
+    count = hidden[0].shape[0]
+    piece = count // 4
+
+    @pl.when(step == 0)
+    def _():
+        for r in range(4):
+            held[r * count : (r + 1) * count, :] = hidden[r][...]
+
+    @pl.when(step < 2)
+    def _():
+        for whole, new in zip(wholes, own_new):
+            whole[...] = new[0]
+
+    for r in range(2):
+        every[r * count : (r + 1) * count, :] = near[r][...]
+
+    @pl.when(step < low_steps)
+    def _():
+        for r in range(2):
+            every[(2 + r) * count : (3 + r) * count, :] = low[r][...]
+
+    @pl.when(step >= low_steps)
+    def _():
+        for r in range(2):
+            for j in range(4):
+                block = lax.rem(at[2] - j + 4, 4)
+                there = pl.ds(pl.multiple_of((2 + r) * count + block * piece, piece), piece)
+                every[there, :] = high[4 * r + j][...]
+
+    product = lax.dot_general(
+        held[...], every[...], (((0,), (0,)), ((), ())), preferred_element_type=jnp.float32
+    )
+    out[...] = (product * norm[0]).astype(jnp.bfloat16)
+
+
+def weight_grad(at, norm, hidden, rows, low, high, own_new):
+    count, block = hidden[0].shape
+    piece, depth = high[0].shape[0], rows.shape[1]
+    low_steps = low[0].shape[1] // OUT_STEP
+    specs = [pl.BlockSpec(memory_space=pltpu.SMEM)]
+    specs += [pl.BlockSpec((count, block), lambda n, at: (0, 0))] * 4
+    specs += [pl.BlockSpec((count, OUT_STEP), lambda n, at, r=r: (r, n)) for r in range(2)]
+    specs += [pl.BlockSpec((count, OUT_STEP), lambda n, at: (0, jnp.minimum(n, low_steps - 1)))] * 2
+    specs += [pl.BlockSpec((piece, OUT_STEP), lambda n, at: (0, jnp.maximum(n - low_steps, 0)))] * 8
+    specs += [pl.BlockSpec((1, count, block), lambda n, at: (jnp.minimum(n, 1), 0, 0))] * 2
+    whole = jax.ShapeDtypeStruct((count, 4 * block), jnp.bfloat16)
+    return pl.pallas_call(
+        functools.partial(weight_grad_kernel, low_steps),
+        grid_spec=pltpu.PrefetchScalarGridSpec(
+            num_scalar_prefetch=1,
+            grid=(depth // OUT_STEP,),
+            in_specs=specs,
+            out_specs=[pl.BlockSpec((count, block), lambda n, at: (0, at[3 + jnp.minimum(n, 1)]))] * 2
+            + [pl.BlockSpec((block, OUT_STEP), lambda n, at: (0, n))],
+            scratch_shapes=[
+                pltpu.VMEM((4 * count, block), jnp.bfloat16),
+                pltpu.VMEM((4 * count, OUT_STEP), jnp.bfloat16),
+            ],
+        ),
+        out_shape=[whole, whole, jax.ShapeDtypeStruct((block, depth), jnp.bfloat16)],
+        compiler_params=pltpu.CompilerParams(vmem_limit_bytes=VMEM_BYTES),
+        cost_estimate=pl.CostEstimate(flops=1000, bytes_accessed=1000, transcendentals=0),
+        name="weight_grad",
+    )(at, norm, *hidden, rows, rows, *low, *high, *own_new)
+
+
+def place_kernel(at, gate, up, earlier_gate, earlier_up, gate_out, up_out):
+    gate_out[...] = gate[...]
+    up_out[...] = up[...]
+
+
+def place_pair(at, news, wholes):
+    count, block = news[0].shape[1:]
+    return pl.pallas_call(
+        place_kernel,
+        grid_spec=pltpu.PrefetchScalarGridSpec(
+            num_scalar_prefetch=1,
+            grid=(2,),
+            in_specs=[pl.BlockSpec((None, count, block), lambda n, at: (n, 0, 0))] * 2
+            + [pl.BlockSpec(memory_space=pl.ANY)] * 2,
+            out_specs=[pl.BlockSpec((count, block), lambda n, at: (0, at[5 + n]))] * 2,
+        ),
+        out_shape=[jax.ShapeDtypeStruct(whole.shape, whole.dtype) for whole in wholes],
+        input_output_aliases={3: 0, 4: 1},
+        compiler_params=pltpu.CompilerParams(vmem_limit_bytes=VMEM_BYTES),
+        cost_estimate=pl.CostEstimate(flops=1000, bytes_accessed=1000, transcendentals=0),
+        name="place_pair",
+    )(at, *news, *wholes)
+
+
+def paired(section_layers, grad_out, gate_act, up_act, down_weight):
+    place, replica = lax.axis_index("tensor"), lax.axis_index("dp")
+    chip, core = replica // 2, replica % 2
+    across = [(0, 2), (1, 3), (2, 0), (3, 1)]
+    pair = [(0, 1), (1, 0), (2, 3), (3, 2)]
+    own_rows = grad_out[0, 0]
+    gate, up, weight = gate_act[0, 0], up_act[0, 0], down_weight[0]
+    rows, width = gate.shape
+    depth = weight.shape[1]
+    block = width // 4
+    mine, theirs = 2 * chip + core, 2 * (1 - chip) + core
+    pair_mine, pair_theirs = 2 * chip + 1 - core, 2 * (1 - chip) + 1 - core
+
+    def to_pair(value):
+        return lax.ppermute(value, "dp", pair)
+
+    def to_across(value):
+        return lax.ppermute(value, "dp", across)
+
+    def around(value, places=1):
+        return lax.ppermute(value, "tensor", [(i, (i + places) % 4) for i in range(4)])
+
+    split = depth * 3 // 8 // OUT_STEP * OUT_STEP
+    at = jnp.stack([core, chip, place, mine, theirs, pair_mine, pair_theirs]).astype(jnp.int32)
+    slots = [own_rows, around(own_rows)]
+    far_b0 = to_across(own_rows[:, split:])
+    near = [to_pair(own_rows)]
+    own_theirs = factors(at, gate, up, block, 4)
+    shared = share(at, gate, up, block, 5)
+
+    slots[1], far_b0, near[0], *shared, far_own = lax.optimization_barrier(
+        (slots[1], far_b0, near[0], *shared, own_theirs[0])
+    )
+    slots.append(around(slots[1]))
+    near.append(to_pair(slots[1]))
+    pair_gate, pair_up = to_pair(shared[0]), to_pair(shared[1])
+    far_own = to_across(far_own)
+    pair_gate, pair_up, near[1] = lax.optimization_barrier((pair_gate, pair_up, near[1]))
+    near_theirs = factors(at, pair_gate, pair_up, block, -2)
+    near_mine = factors(at, pair_gate, pair_up, block, -1)
+
+    slots[2], far_near, gate, section_layers, _ = lax.optimization_barrier(
+        (slots[2], near_theirs[0], gate, section_layers, near_mine[0])
+    )
+    scale = section_scale(section_layers).reshape(1)
+    norm = scale / jnp.sqrt(jnp.float32(rows * 4))
+    slots.append(around(slots[2]))
+    near.append(to_pair(slots[2]))
+    cross_b = [to_pair(after(far_b0, slots[2]))]
+    far_near = to_across(far_near)
+    own_mine = factors(at, gate, up, block, 3)
+    part = assemble(at, slots[:3], split)
+
+    slots[3], near[2], cross_b[0], far_own, part, scale, norm, _ = lax.optimization_barrier(
+        (slots[3], near[2], cross_b[0], far_own, part, scale, norm, own_mine[0])
+    )
+    near.append(to_pair(slots[3]))
+    far_a = to_across(complete(at, slots[3], part))
+    far_b = [far_b0] + [around(after(far_b0, slots[3]), places) for places in (1, 2, 3)]
+
+    own_gate, own_up, near_gate, near_up, rows_here = hidden_grad(
+        at, scale, [*slots, *near], weight,
+        [own_mine[1:], own_theirs[1:], near_mine[1:], near_theirs[1:]], 0, block,
+    )
+    near_gate, near_up, far_near, far_a, *far_b = lax.optimization_barrier(
+        (near_gate, near_up, far_near, far_a, *far_b)
+    )
+    cross_a = to_pair(far_a)
+    cross_b += [to_pair(slot) for slot in far_b[1:]]
+    near_gate, near_up, cross_a, *cross_b = lax.optimization_barrier(
+        (near_gate, near_up, cross_a, *cross_b)
+    )
+    from_pair = [to_pair(near_gate), to_pair(near_up)]
+
+    hidden = [own_mine[0], near_mine[0], far_own, far_near]
+    grad_gate, grad_up, grad_down_w = weight_grad(
+        at, norm, hidden, rows_here, [far_a, cross_a], [*far_b, *cross_b], [own_gate, own_up]
+    )
+    grad_gate, grad_up = place_pair(at, from_pair, [grad_gate, grad_up])
+    return (grad_gate[None, None], grad_up[None, None], grad_down_w[None])
 
 
 def solution(mesh):
+    def per_device(section_layers, grad_out, gate_act, up_act, down_weight):
+        sizes = (grad_out.shape[2] % 16, gate_act.shape[3] % 1024, grad_out.shape[3] % 1024)
+        small = mesh.shape["tensor"] == 4 and mesh.shape["dp"] == 4
+        form = paired if small and sizes == (0, 0, 0) else general
+        return form(section_layers, grad_out, gate_act, up_act, down_weight)
+
     placed = (
         P(),
         P("pipe", "dp", "tensor", None),

time: 132 us -> 101 us (0.77)
  Pallas kernels: 0 us -> 67.1 us
  waiting for transfers between devices: 59.3 us -> 10.8 us
  matrix products: 47.2 us -> 0 us
  local copies, waits for them, and re-layouts: 13.5 us -> 5.3 us
  starting transfers between devices: 7.99 us -> 14.1 us
    pallas_call x0 -> x10, Pallas kernels: none -> 67.1 us  [the longest x1 21.6 us: hidden_grad(): pl.pallas_call(hidden_grad_kernel, grid_spec=pltpu.PrefetchScalarGridSpec...]
    ppermute x12 -> x23, waiting for transfers between devices: 59.3 us -> 10.8 us  [the longest x13 5.88 us: to_pair(): return lax.ppermute(value, 'dp', pair)]
    dot_general x2 -> x0, matrix products: 47.2 us -> none  [the longest x1 30.5 us: per_device(): lax.dot_general(all_rows, weight, (((1,), (1,)), ((), ())), preferred_ele...]
    dynamic_update_slice x8 -> x0, local copies, waits for them, and re-layouts: 7.26 us -> none  [in_order(): whole = lax.dynamic_update_slice(whole, slot, (block * rows, 0))]
    ppermute x12 -> x23, starting transfers between devices: 7.99 us -> 14.1 us  [the longest x4 6.08 us: to_across(): return lax.ppermute(value, 'dp', across)]
    unnamed x0 -> x42, local copies, waits for them, and re-layouts: none -> 3.7 us
    dynamic_slice x3 -> x0, local copies, waits for them, and re-layouts: 3.57 us -> none  [the longest x2 2.17 us: columns_of(): return lax.dynamic_slice(hidden, (0, owner * block), (rows, block * count))]
    another operation x2 -> x1, local copies, waits for them, and re-layouts: 2.67 us -> 0.61 us  [paired(): jnp.stack([core, chip, place, mine, theirs, pair_mine, pair_theirs])]
  transfers between devices with their start and end apart: 12 -> 23, of which waited for: 7 -> 7; matrix products, arithmetic and copies ran while one was open for 34% -> 2% of each run, Pallas kernels for 0% -> 63%
where the time goes in v2:
time: 101 us; the launch traced here: 100 us
  Pallas kernels  67.1 us (66%)
  starting transfers between devices  14.1 us (14%)
  waiting for transfers between devices  10.8 us (11%)
  local copies, waits for them, and re-layouts  5.3 us (5%)
  between operations  2.2 us (2%)
    pallas_call x1, Pallas kernels, hidden_grad(): pl.pallas_call(hidden_grad_kernel, grid_spec=pltpu.PrefetchScalarGridSpec...  21.6 us
    pallas_call x1, Pallas kernels, weight_grad(): pl.pallas_call(functools.partial(weight_grad_kernel, low_steps), grid_spe...  19.5 us
    pallas_call x4, Pallas kernels, factors(): pl.pallas_call(factors_kernel, grid_spec=pltpu.PrefetchScalarGridSpec(num...  13.9 us
    ppermute x4, starting transfers between devices, to_across(): return lax.ppermute(value, 'dp', across)  6.08 us
    ppermute x13, waiting for transfers between devices, to_pair(): return lax.ppermute(value, 'dp', pair)  5.88 us
    ppermute x6, waiting for transfers between devices, around(): lax.ppermute(value, 'tensor', [(i, (i + places) % 4) for i in range(4)])  4.93 us
    ppermute x6, starting transfers between devices, around(): lax.ppermute(value, 'tensor', [(i, (i + places) % 4) for i in range(4)])  4.78 us
    unnamed x42, local copies, waits for them, and re-layouts  3.7 us
  transfers between devices with their start and end apart: 23, of which 7 were waited for; matrix products, arithmetic and copies ran while one was open for 2% of the time, Pallas kernels for 63%

profile of v2, /device:TPU:0, one launch (start us, length us, event | category | flops | bytes accessed | tf_op | source)
XLA Modules:
  0.0 100.2 jit_solution(6310211517968162631)
XLA Ops:
  0.6 0.5 collective-permute-start.2
  1.1 2.6 %collective-permute-start = (bf16[48,4096]{1,0:T(8,128)(2,1)}, bf16[48,4096]{1,0:T(8,128)(2,1)S(1)}, u32[]{:S(2)}, u32[]{:S(2)}) collective-permute-start(bf16[48,4096]{1,0:T(8,128)(2,1)} %bitcast.25), channel_id=1, source_target_pairs={{0,4},{4,8},{8,12},{12,0},{1,5},{5,9},{9,13},{13,1},{2,6},{6,10},{... | collective-permute-start | bytes 1179656 | tf_op jit(solution)/shard_map/ppermute | solution.py:380
  3.8 1.0 slice.4
  4.8 1.6 %collective-permute-start.1 = (bf16[48,2560]{1,0:T(8,128)(2,1)S(1)}, bf16[48,2560]{1,0:T(8,128)(2,1)}, u32[]{:S(2)}, u32[]{:S(2)}) collective-permute-start(bf16[48,2560]{1,0:T(8,128)(2,1)S(1)} %slice.4), channel_id=1, source_target_pairs={{0,2},{1,3},{2,0},{3,1},{4,6},{5,7},{6,4},{7,5},{8,10},{9,11},{10,... | collective-permute-start | bytes 737288 | tf_op jit(solution)/shard_map/ppermute | solution.py:377
  6.4 0.6 stack.31.at
  7.0 3.5 %factors.4 = (bf16[192,1792]{1,0:T(8,128)(2,1)}, bf16[192,1792]{1,0:T(8,128)(2,1)}, bf16[192,1792]{1,0:T(8,128)(2,1)}) custom-call(s32[7]{0:T(128)} %stack.31.at, bf16[192,7168]{1,0:T(8,128)(2,1)} %bitcast.16, bf16[192,7168]{1,0:T(8,128)(2,1)} %bitcast.19), custom_call_target="tpu_custom_call" | custom-call | flops 1000 | bytes 1000 | tf_op jit(solution)/shard_map/factors/pallas_call | solution.py:113
  10.4 3.6 %share.1 = (bf16[192,3584]{1,0:T(8,128)(2,1)}, bf16[192,3584]{1,0:T(8,128)(2,1)}) custom-call(s32[7]{0:T(128)} %stack.31.at, bf16[192,7168]{1,0:T(8,128)(2,1)} %bitcast.17, bf16[192,7168]{1,0:T(8,128)(2,1)} %bitcast.20), custom_call_target="tpu_custom_call" | custom-call | flops 1000 | bytes 1000 | tf_op jit(solution)/shard_map/share/pallas_call | solution.py:188
  14.1 1.7 %collective-permute-done.refs_1_ = bf16[48,4096]{1,0:T(8,128)(2,1)S(1)} collective-permute-done((bf16[48,4096]{1,0:T(8,128)(2,1)}, bf16[48,4096]{1,0:T(8,128)(2,1)S(1)}, u32[]{:S(2)}, u32[]{:S(2)}) %collective-permute-start) | collective-permute-done | bytes 393248 | tf_op jit(solution)/shard_map/ppermute | solution.py:380
  15.7 0.5 collective-permute-start.5
  16.3 0.0 collective-permute-start.6
  16.3 0.1 collective-permute-start.3
  16.3 1.5 %collective-permute-start.10 = (bf16[192,1792]{1,0:T(8,128)(2,1)}, bf16[192,1792]{1,0:T(8,128)(2,1)S(1)}, u32[]{:S(2)}, u32[]{:S(2)}) collective-permute-start(bf16[192,1792]{1,0:T(8,128)(2,1)} %get-tuple-element.77), channel_id=1, source_target_pairs={{0,2},{1,3},{2,0},{3,1},{4,6},{5,7},{6,4},{7,5},{8,10},{9,11},{10,... | collective-permute-start | bytes 2064392 | tf_op jit(solution)/shard_map/ppermute | solution.py:377
  17.8 2.2 %collective-permute-done.6.refs_5_ = bf16[48,4096]{1,0:T(8,128)(2,1)S(1)} collective-permute-done((bf16[48,4096]{1,0:T(8,128)(2,1)S(1)}, bf16[48,4096]{1,0:T(8,128)(2,1)S(1)}, u32[]{:S(2)}, u32[]{:S(2)}) %collective-permute-start.6) | collective-permute-done | bytes 393248 | tf_op jit(solution)/shard_map/ppermute | solution.py:374
  20.0 0.0 collective-permute-done.4.gate
  20.0 1.6 %collective-permute-done.5.up = bf16[192,3584]{1,0:T(8,128)(2,1)S(1)} collective-permute-done((bf16[192,3584]{1,0:T(8,128)(2,1)}, bf16[192,3584]{1,0:T(8,128)(2,1)S(1)}, u32[]{:S(2)}, u32[]{:S(2)}) %collective-permute-start.5) | collective-permute-done | bytes 1376288 | tf_op jit(solution)/shard_map/ppermute | solution.py:374
  21.6 1.1 %copy-done.1 = bf16[192,3584]{1,0:T(8,128)(2,1)} copy-done((bf16[192,3584]{1,0:T(8,128)(2,1)}, bf16[192,3584]{1,0:T(8,128)(2,1)S(1)}, u32[]{:S(2)}) %copy-start.1) | copy-done | bytes 1376280
  22.7 3.5 %factors.6 = (bf16[192,1792]{1,0:T(8,128)(2,1)}, bf16[192,1792]{1,0:T(8,128)(2,1)}, bf16[192,1792]{1,0:T(8,128)(2,1)}) custom-call(s32[7]{0:T(128)} %stack.31.at, bf16[192,3584]{1,0:T(8,128)(2,1)} %copy-done, bf16[192,3584]{1,0:T(8,128)(2,1)} %copy-done.1), custom_call_target="tpu_custom_call" | custom-call | flops 1000 | bytes 1000 | tf_op jit(solution)/shard_map/factors/pallas_call | solution.py:113
  26.2 3.6 %factors.5 = (bf16[192,1792]{1,0:T(8,128)(2,1)}, bf16[192,1792]{1,0:T(8,128)(2,1)}, bf16[192,1792]{1,0:T(8,128)(2,1)}) custom-call(s32[7]{0:T(128)} %stack.31.at, bf16[192,3584]{1,0:T(8,128)(2,1)} %copy-done, bf16[192,3584]{1,0:T(8,128)(2,1)} %copy-done.1), custom_call_target="tpu_custom_call" | custom-call | flops 1000 | bytes 1000 | tf_op jit(solution)/shard_map/factors/pallas_call | solution.py:113
  29.8 0.0 collective-permute-done.3.refs_2_
  29.8 0.2 collective-permute-start.8
  30.0 0.0 collective-permute-start.7
  30.0 0.4 collective-permute-start.9
  30.3 1.5 %collective-permute-start.12 = (bf16[192,1792]{1,0:T(8,128)(2,1)}, bf16[192,1792]{1,0:T(8,128)(2,1)S(1)}, u32[]{:S(2)}, u32[]{:S(2)}) collective-permute-start(bf16[192,1792]{1,0:T(8,128)(2,1)} %get-tuple-element.96), channel_id=1, source_target_pairs={{0,2},{1,3},{2,0},{3,1},{4,6},{5,7},{6,4},{7,5},{8,10},{9,11},{10,... | collective-permute-start | bytes 2064392 | tf_op jit(solution)/shard_map/ppermute | solution.py:377
  31.9 0.7 fusion.1
  32.5 2.6 %assemble.1.earlier = bf16[192,1536]{1,0:T(8,128)(2,1)} custom-call(s32[7]{0:T(128)} %stack.31.at, bf16[48,4096]{1,0:T(8,128)(2,1)} %bitcast.27, bf16[48,4096]{1,0:T(8,128)(2,1)} %copy-done.3, bf16[48,4096]{1,0:T(8,128)(2,1)} %copy-done.4), custom_call_target="tpu_custom_call" | custom-call | flops 1000 | bytes 1000 | tf_op jit(solution)/shard_map/assemble/pallas_call | solution.py:139
  35.1 3.4 %factors.7 = (bf16[192,1792]{1,0:T(8,128)(2,1)}, bf16[192,1792]{1,0:T(8,128)(2,1)}, bf16[192,1792]{1,0:T(8,128)(2,1)}) custom-call(s32[7]{0:T(128)} %stack.31.at, bf16[192,7168]{1,0:T(8,128)(2,1)} %bitcast.18, bf16[192,7168]{1,0:T(8,128)(2,1)} %bitcast.21), custom_call_target="tpu_custom_call" | custom-call | flops 1000 | bytes 1000 | tf_op jit(solution)/shard_map/factors/pallas_call | solution.py:113
  39.9 0.0 collective-permute-done.8.refs_6_
  39.9 3.3 %collective-permute-done.7.refs_3_.slot = bf16[48,4096]{1,0:T(8,128)(2,1)S(1)} collective-permute-done((bf16[48,4096]{1,0:T(8,128)(2,1)S(1)}, bf16[48,4096]{1,0:T(8,128)(2,1)S(1)}, u32[]{:S(2)}, u32[]{:S(2)}) %collective-permute-start.7) | collective-permute-done | bytes 393248 | tf_op jit(solution)/shard_map/ppermute | solution.py:380
  43.2 0.7 copy-done.2
  43.9 2.2 %complete.1 = bf16[192,1536]{1,0:T(8,128)(2,1)} custom-call(s32[7]{0:T(128)} %stack.31.at, bf16[48,4096]{1,0:T(8,128)(2,1)} %copy-done.2, bf16[192,1536]{1,0:T(8,128)(2,1)} %assemble.1.earlier), custom_call_target="tpu_custom_call", output_to_operand_aliasing={{}: (2, {})} | custom-call | flops 1000 | bytes 1000 | tf_op jit(solution)/shard_map/complete/pallas_call | solution.py:160
  46.1 1.5 %collective-permute-start.13 = (bf16[192,1536]{1,0:T(8,128)(2,1)}, bf16[192,1536]{1,0:T(8,128)(2,1)S(1)}, u32[]{:S(2)}, u32[]{:S(2)}) collective-permute-start(bf16[192,1536]{1,0:T(8,128)(2,1)} %complete.1), channel_id=1, source_target_pairs={{0,2},{1,3},{2,0},{3,1},{4,6},{5,7},{6,4},{7,5},{8,10},{9,11},{10,... | collective-permute-start | bytes 1769480 | tf_op jit(solution)/shard_map/ppermute | solution.py:377
  47.7 2.1 %collective-permute-start.14 = (bf16[48,2560]{1,0:T(8,128)(2,1)}, bf16[48,2560]{1,0:T(8,128)(2,1)S(1)}, u32[]{:S(2)}, u32[]{:S(2)}) collective-permute-start(bf16[48,2560]{1,0:T(8,128)(2,1)} %collective-permute-done.1.refs_8_), channel_id=1, source_target_pairs={{0,4},{4,8},{8,12},{12,0},{1,5},{5,9},{9,13},{13,1},{2,6},{6,10},{... | collective-permute-start | bytes 737288 | tf_op jit(solution)/shard_map/ppermute | solution.py:380
  49.8 21.6 %hidden_grad.1 = (bf16[2,192,1792]{2,1,0:T(8,128)(2,1)}, bf16[2,192,1792]{2,1,0:T(8,128)(2,1)}, bf16[2,192,1792]{2,1,0:T(8,128)(2,1)}, bf16[2,192,1792]{2,1,0:T(8,128)(2,1)}, bf16[384,4096]{1,0:T(8,128)(2,1)}) custom-call(s32[7]{0:T(128)} %stack.31.at, f32[1]{0:T(128)} %bitcast.10.scale, bf16[48,4096]{1,0:T(8,128)(2,1)} %bitcast.28, ...), custom_call_target="tpu_custom_call" | custom-call | flops 1000 | bytes 1000 | tf_op jit(solution)/shard_map/hidden_grad/pallas_call | solution.py:242
  71.5 0.1 collective-permute-start.17
  71.5 0.5 collective-permute-start.18
  72.0 0.1 collective-permute-start.19
  72.1 0.4 collective-permute-start.20
  72.5 1.3 %collective-permute-done.18.refs_13_ = bf16[48,2560]{1,0:T(8,128)(2,1)S(1)} collective-permute-done((bf16[48,2560]{1,0:T(8,128)(2,1)S(1)}, bf16[48,2560]{1,0:T(8,128)(2,1)S(1)}, u32[]{:S(2)}, u32[]{:S(2)}) %collective-permute-start.18) | collective-permute-done | bytes 245792 | tf_op jit(solution)/shard_map/ppermute | solution.py:374
  73.9 0.3 collective-permute-done.19.refs_14_
  74.2 0.3 collective-permute-done.20.refs_15_
  74.6 0.1 collective-permute-start.21
  74.7 0.4 collective-permute-start.22
  75.2 0.1 copy-done.19
  75.3 0.2 copy-done.10
  75.5 19.5 %weight_grad.1 = (bf16[192,7168]{1,0:T(8,128)(2,1)}, bf16[192,7168]{1,0:T(8,128)(2,1)}, bf16[1792,4096]{1,0:T(8,128)(2,1)}) custom-call(s32[7]{0:T(128)} %stack.31.at, f32[1]{0:T(128)S(6)} %div.18.norm, bf16[192,1792]{1,0:T(8,128)(2,1)} %get-tuple-element.80.refs_0_, bf16[192,1792]{1,0:T(8,128)(2,1)} %get-tuple-element.73.refs_1_, ...), custom_call_target="tpu_custom_call" | custom-call | flops 1000 | bytes 1000 | tf_op jit(solution)/shard_map/weight_grad/pallas_call | solution.py:316
  95.1 1.1 %copy-done.5 = bf16[2,192,1792]{2,1,0:T(8,128)(2,1)} copy-done((bf16[2,192,1792]{2,1,0:T(8,128)(2,1)}, bf16[2,192,1792]{2,1,0:T(8,128)(2,1)S(1)}, u32[]{:S(2)}) %copy-start.5) | copy-done | bytes 1376280
  96.2 0.4 copy-done.6
  96.6 3.6 %place_pair.1 = (bf16[192,7168]{1,0:T(8,128)(2,1)}, bf16[192,7168]{1,0:T(8,128)(2,1)}) custom-call(s32[7]{0:T(128)} %stack.31.at, bf16[2,192,1792]{2,1,0:T(8,128)(2,1)} %copy-done.5, bf16[2,192,1792]{2,1,0:T(8,128)(2,1)} %copy-done.6, bf16[192,7168]{1,0:T(8,128)(2,1)} %get-tuple-element.120.earlier_gate, ...), custom_call_target="tpu_custom_call", output_to_operand_aliasing={{0}: (3, {}), {1}: (4, {})} | custom-call | flops 1000 | bytes 1000 | tf_op jit(solution)/shard_map/place_pair/pallas_call | solution.py:343
  (53 shorter events, 0.1 us)
Async XLA Ops:
  0.6 13.4 %collective-permute-start.2 = (bf16[48,4096]{1,0:T(8,128)(2,1)}, bf16[48,4096]{1,0:T(8,128)(2,1)S(1)}, u32[]{:S(2)}, u32[]{:S(2)}) collective-permute-start(bf16[48,4096]{1,0:T(8,128)(2,1)} %bitcast.24), channel_id=1, source_target_pairs={{0,1},{1,0},{2,3},{3,2},{4,5},{5,4},{6,7},{7,6},{8,9},{9,8},{10,11... | collective-permute-start | bytes 1179656 | tf_op jit(solution)/shard_map/ppermute | solution.py:374
  1.1 14.6 %collective-permute-start = (bf16[48,4096]{1,0:T(8,128)(2,1)}, bf16[48,4096]{1,0:T(8,128)(2,1)S(1)}, u32[]{:S(2)}, u32[]{:S(2)}) collective-permute-start(bf16[48,4096]{1,0:T(8,128)(2,1)} %bitcast.25), channel_id=1, source_target_pairs={{0,4},{4,8},{8,12},{12,0},{1,5},{5,9},{9,13},{13,1},{2,6},{6,10},{... | collective-permute-start | bytes 1179656 | tf_op jit(solution)/shard_map/ppermute | solution.py:380
  4.8 9.3 %collective-permute-start.1 = (bf16[48,2560]{1,0:T(8,128)(2,1)S(1)}, bf16[48,2560]{1,0:T(8,128)(2,1)}, u32[]{:S(2)}, u32[]{:S(2)}) collective-permute-start(bf16[48,2560]{1,0:T(8,128)(2,1)S(1)} %slice.4), channel_id=1, source_target_pairs={{0,2},{1,3},{2,0},{3,1},{4,6},{5,7},{6,4},{7,5},{8,10},{9,11},{10,... | collective-permute-start | bytes 737288 | tf_op jit(solution)/shard_map/ppermute | solution.py:377
  14.1 24.5 %copy-start.11 = (bf16[48,4096]{1,0:T(8,128)(2,1)}, bf16[48,4096]{1,0:T(8,128)(2,1)S(1)}, u32[]{:S(2)}) copy-start(bf16[48,4096]{1,0:T(8,128)(2,1)S(1)} %collective-permute-done.2.refs_4_) | copy-start | bytes 1179652
  15.7 16.8 %copy-start.3 = (bf16[48,4096]{1,0:T(8,128)(2,1)}, bf16[48,4096]{1,0:T(8,128)(2,1)S(1)}, u32[]{:S(2)}) copy-start(bf16[48,4096]{1,0:T(8,128)(2,1)S(1)} %collective-permute-done.refs_1_) | copy-start | bytes 1179652
  15.7 4.3 %collective-permute-start.4 = (bf16[192,3584]{1,0:T(8,128)(2,1)}, bf16[192,3584]{1,0:T(8,128)(2,1)S(1)}, u32[]{:S(2)}, u32[]{:S(2)}) collective-permute-start(bf16[192,3584]{1,0:T(8,128)(2,1)} %get-tuple-element.68), channel_id=1, source_target_pairs={{0,1},{1,0},{2,3},{3,2},{4,5},{5,4},{6,7},{7,6},{8,9},{9,8},{10,11... | collective-permute-start | bytes 4128776 | tf_op jit(solution)/shard_map/ppermute | solution.py:374
  15.7 5.9 %collective-permute-start.5 = (bf16[192,3584]{1,0:T(8,128)(2,1)}, bf16[192,3584]{1,0:T(8,128)(2,1)S(1)}, u32[]{:S(2)}, u32[]{:S(2)}) collective-permute-start(bf16[192,3584]{1,0:T(8,128)(2,1)} %get-tuple-element.69), channel_id=1, source_target_pairs={{0,1},{1,0},{2,3},{3,2},{4,5},{5,4},{6,7},{7,6},{8,9},{9,8},{10,11... | collective-permute-start | bytes 4128776 | tf_op jit(solution)/shard_map/ppermute | solution.py:374
  16.3 3.7 %collective-permute-start.6 = (bf16[48,4096]{1,0:T(8,128)(2,1)S(1)}, bf16[48,4096]{1,0:T(8,128)(2,1)S(1)}, u32[]{:S(2)}, u32[]{:S(2)}) collective-permute-start(bf16[48,4096]{1,0:T(8,128)(2,1)S(1)} %collective-permute-done.refs_1_), channel_id=1, source_target_pairs={{0,1},{1,0},{2,3},{3,2},{4,5},{5,4},{6,7},{7,6},{8,9},{9,8},{10,11... | collective-permute-start | bytes 1179656 | tf_op jit(solution)/shard_map/ppermute | solution.py:374
  16.3 13.5 %collective-permute-start.3 = (bf16[48,4096]{1,0:T(8,128)(2,1)S(1)}, bf16[48,4096]{1,0:T(8,128)(2,1)S(1)}, u32[]{:S(2)}, u32[]{:S(2)}) collective-permute-start(bf16[48,4096]{1,0:T(8,128)(2,1)S(1)} %collective-permute-done.refs_1_), channel_id=1, source_target_pairs={{0,4},{4,8},{8,12},{12,0},{1,5},{5,9},{9,13},{13,1},{2,6},{6,10},{... | collective-permute-start | bytes 1179656 | tf_op jit(solution)/shard_map/ppermute | solution.py:380
  16.3 23.5 %collective-permute-start.10 = (bf16[192,1792]{1,0:T(8,128)(2,1)}, bf16[192,1792]{1,0:T(8,128)(2,1)S(1)}, u32[]{:S(2)}, u32[]{:S(2)}) collective-permute-start(bf16[192,1792]{1,0:T(8,128)(2,1)} %get-tuple-element.77), channel_id=1, source_target_pairs={{0,2},{1,3},{2,0},{3,1},{4,6},{5,7},{6,4},{7,5},{8,10},{9,11},{10,... | collective-permute-start | bytes 2064392 | tf_op jit(solution)/shard_map/ppermute | solution.py:377
  20.0 18.6 %copy-start.12 = (bf16[48,4096]{1,0:T(8,128)(2,1)}, bf16[48,4096]{1,0:T(8,128)(2,1)S(1)}, u32[]{:S(2)}) copy-start(bf16[48,4096]{1,0:T(8,128)(2,1)S(1)} %collective-permute-done.6.refs_5_) | copy-start | bytes 1179652
  20.0 1.6 %copy-start = (bf16[192,3584]{1,0:T(8,128)(2,1)}, bf16[192,3584]{1,0:T(8,128)(2,1)S(1)}, u32[]{:S(2)}) copy-start(bf16[192,3584]{1,0:T(8,128)(2,1)S(1)} %collective-permute-done.4.gate) | copy-start | bytes 4128772
  21.6 1.1 %copy-start.1 = (bf16[192,3584]{1,0:T(8,128)(2,1)}, bf16[192,3584]{1,0:T(8,128)(2,1)S(1)}, u32[]{:S(2)}) copy-start(bf16[192,3584]{1,0:T(8,128)(2,1)S(1)} %collective-permute-done.5.up) | copy-start | bytes 4128772
  26.2 5.7 %copy-start.20 = (s32[2]{0:T(128)S(1)}, s32[2]{0:T(128)}, u32[]{:S(2)}) copy-start(s32[2]{0:T(128)} %param.5) | copy-start | bytes 28
  29.8 2.8 %copy-start.4 = (bf16[48,4096]{1,0:T(8,128)(2,1)}, bf16[48,4096]{1,0:T(8,128)(2,1)S(1)}, u32[]{:S(2)}) copy-start(bf16[48,4096]{1,0:T(8,128)(2,1)S(1)} %collective-permute-done.3.refs_2_) | copy-start | bytes 1179652
  29.8 10.1 %collective-permute-start.8 = (bf16[48,4096]{1,0:T(8,128)(2,1)S(1)}, bf16[48,4096]{1,0:T(8,128)(2,1)}, u32[]{:S(2)}, u32[]{:S(2)}) collective-permute-start(bf16[48,4096]{1,0:T(8,128)(2,1)S(1)} %collective-permute-done.3.refs_2_), channel_id=1, source_target_pairs={{0,1},{1,0},{2,3},{3,2},{4,5},{5,4},{6,7},{7,6},{8,9},{9,8},{10,11... | collective-permute-start | bytes 1179656 | tf_op jit(solution)/shard_map/ppermute | solution.py:374
  30.0 13.2 %collective-permute-start.7 = (bf16[48,4096]{1,0:T(8,128)(2,1)S(1)}, bf16[48,4096]{1,0:T(8,128)(2,1)S(1)}, u32[]{:S(2)}, u32[]{:S(2)}) collective-permute-start(bf16[48,4096]{1,0:T(8,128)(2,1)S(1)} %collective-permute-done.3.refs_2_), channel_id=1, source_target_pairs={{0,4},{4,8},{8,12},{12,0},{1,5},{5,9},{9,13},{13,1},{2,6},{6,10},{... | collective-permute-start | bytes 1179656 | tf_op jit(solution)/shard_map/ppermute | solution.py:380
  30.0 9.9 %collective-permute-start.9 = (bf16[48,2560]{1,0:T(8,128)(2,1)}, bf16[48,2560]{1,0:T(8,128)(2,1)}, u32[]{:S(2)}, u32[]{:S(2)}) collective-permute-start(bf16[48,2560]{1,0:T(8,128)(2,1)} %collective-permute-done.1.refs_8_), channel_id=1, source_target_pairs={{0,1},{1,0},{2,3},{3,2},{4,5},{5,4},{6,7},{7,6},{8,9},{9,8},{10,11... | collective-permute-start | bytes 737288 | tf_op jit(solution)/shard_map/ppermute | solution.py:374
  30.3 41.1 %collective-permute-start.12 = (bf16[192,1792]{1,0:T(8,128)(2,1)}, bf16[192,1792]{1,0:T(8,128)(2,1)S(1)}, u32[]{:S(2)}, u32[]{:S(2)}) collective-permute-start(bf16[192,1792]{1,0:T(8,128)(2,1)} %get-tuple-element.96), channel_id=1, source_target_pairs={{0,2},{1,3},{2,0},{3,1},{4,6},{5,7},{6,4},{7,5},{8,10},{9,11},{10,... | collective-permute-start | bytes 2064392 | tf_op jit(solution)/shard_map/ppermute | solution.py:377
  39.9 31.5 %copy-start.7 = (bf16[192,1792]{1,0:T(8,128)(2,1)}, bf16[192,1792]{1,0:T(8,128)(2,1)S(1)}, u32[]{:S(2)}) copy-start(bf16[192,1792]{1,0:T(8,128)(2,1)S(1)} %collective-permute-done.10.refs_2_) | copy-start | bytes 2064388
  43.2 0.7 copy-start.2
  43.2 4.5 %collective-permute-start.11 = (bf16[48,4096]{1,0:T(8,128)(2,1)S(1)}, bf16[48,4096]{1,0:T(8,128)(2,1)S(1)}, u32[]{:S(2)}, u32[]{:S(2)}) collective-permute-start(bf16[48,4096]{1,0:T(8,128)(2,1)S(1)} %collective-permute-done.7.refs_3_.slot), channel_id=1, source_target_pairs={{0,1},{1,0},{2,3},{3,2},{4,5},{5,4},{6,7},{7,6},{8,9},{9,8},{10,11... | collective-permute-start | bytes 1179656 | tf_op jit(solution)/shard_map/ppermute | solution.py:374
  46.1 25.3 %collective-permute-start.13 = (bf16[192,1536]{1,0:T(8,128)(2,1)}, bf16[192,1536]{1,0:T(8,128)(2,1)S(1)}, u32[]{:S(2)}, u32[]{:S(2)}) collective-permute-start(bf16[192,1536]{1,0:T(8,128)(2,1)} %complete.1), channel_id=1, source_target_pairs={{0,2},{1,3},{2,0},{3,1},{4,6},{5,7},{6,4},{7,5},{8,10},{9,11},{10,... | collective-permute-start | bytes 1769480 | tf_op jit(solution)/shard_map/ppermute | solution.py:377
  47.7 23.7 %collective-permute-start.16 = (bf16[48,2560]{1,0:T(8,128)(2,1)}, bf16[48,2560]{1,0:T(8,128)(2,1)S(1)}, u32[]{:S(2)}, u32[]{:S(2)}) collective-permute-start(bf16[48,2560]{1,0:T(8,128)(2,1)} %collective-permute-done.1.refs_8_), channel_id=1, source_target_pairs={{0,12},{4,0},{8,4},{12,8},{1,13},{5,1},{9,5},{13,9},{2,14},{6,2},{... | collective-permute-start | bytes 737288 | tf_op jit(solution)/shard_map/ppermute | solution.py:380
  47.7 23.7 %collective-permute-start.15 = (bf16[48,2560]{1,0:T(8,128)(2,1)}, bf16[48,2560]{1,0:T(8,128)(2,1)S(1)}, u32[]{:S(2)}, u32[]{:S(2)}) collective-permute-start(bf16[48,2560]{1,0:T(8,128)(2,1)} %collective-permute-done.1.refs_8_), channel_id=1, source_target_pairs={{0,8},{4,12},{8,0},{12,4},{1,9},{5,13},{9,1},{13,5},{2,10},{6,14},... | collective-permute-start | bytes 737288 | tf_op jit(solution)/shard_map/ppermute | solution.py:380
  47.7 2.1 %copy-start.13 = (bf16[48,4096]{1,0:T(8,128)(2,1)}, bf16[48,4096]{1,0:T(8,128)(2,1)S(1)}, u32[]{:S(2)}) copy-start(bf16[48,4096]{1,0:T(8,128)(2,1)S(1)} %collective-permute-done.11.refs_7_) | copy-start | bytes 1179652
  47.7 23.7 %collective-permute-start.14 = (bf16[48,2560]{1,0:T(8,128)(2,1)}, bf16[48,2560]{1,0:T(8,128)(2,1)S(1)}, u32[]{:S(2)}, u32[]{:S(2)}) collective-permute-start(bf16[48,2560]{1,0:T(8,128)(2,1)} %collective-permute-done.1.refs_8_), channel_id=1, source_target_pairs={{0,4},{4,8},{8,12},{12,0},{1,5},{5,9},{9,13},{13,1},{2,6},{6,10},{... | collective-permute-start | bytes 737288 | tf_op jit(solution)/shard_map/ppermute | solution.py:380
  71.4 3.8 %copy-start.14 = (bf16[48,2560]{1,0:T(8,128)(2,1)}, bf16[48,2560]{1,0:T(8,128)(2,1)S(1)}, u32[]{:S(2)}) copy-start(bf16[48,2560]{1,0:T(8,128)(2,1)S(1)} %collective-permute-done.16.refs_11_) | copy-start | bytes 737284
  71.4 3.8 %copy-start.15 = (bf16[48,2560]{1,0:T(8,128)(2,1)}, bf16[48,2560]{1,0:T(8,128)(2,1)S(1)}, u32[]{:S(2)}) copy-start(bf16[48,2560]{1,0:T(8,128)(2,1)S(1)} %collective-permute-done.15.refs_10_) | copy-start | bytes 737284
  71.4 3.8 %copy-start.16 = (bf16[48,2560]{1,0:T(8,128)(2,1)}, bf16[48,2560]{1,0:T(8,128)(2,1)S(1)}, u32[]{:S(2)}) copy-start(bf16[48,2560]{1,0:T(8,128)(2,1)S(1)} %collective-permute-done.14.refs_9_) | copy-start | bytes 737284
  71.4 3.7 %copy-start.8 = (bf16[192,1792]{1,0:T(8,128)(2,1)}, bf16[192,1792]{1,0:T(8,128)(2,1)S(1)}, u32[]{:S(2)}) copy-start(bf16[192,1792]{1,0:T(8,128)(2,1)S(1)} %collective-permute-done.12.refs_3_) | copy-start | bytes 2064388
  71.4 3.7 %copy-start.9 = (bf16[192,1536]{1,0:T(8,128)(2,1)}, bf16[192,1536]{1,0:T(8,128)(2,1)S(1)}, u32[]{:S(2)}) copy-start(bf16[192,1536]{1,0:T(8,128)(2,1)S(1)} %collective-permute-done.13.refs_6_) | copy-start | bytes 1769476
  71.5 3.1 %collective-permute-start.17 = (bf16[192,1536]{1,0:T(8,128)(2,1)S(1)}, bf16[192,1536]{1,0:T(8,128)(2,1)S(1)}, u32[]{:S(2)}, u32[]{:S(2)}) collective-permute-start(bf16[192,1536]{1,0:T(8,128)(2,1)S(1)} %collective-permute-done.13.refs_6_), channel_id=1, source_target_pairs={{0,1},{1,0},{2,3},{3,2},{4,5},{5,4},{6,7},{7,6},{8,9},{9,8},{10,11... | collective-permute-start | bytes 1769480 | tf_op jit(solution)/shard_map/ppermute | solution.py:374
  71.5 2.3 %collective-permute-start.18 = (bf16[48,2560]{1,0:T(8,128)(2,1)S(1)}, bf16[48,2560]{1,0:T(8,128)(2,1)S(1)}, u32[]{:S(2)}, u32[]{:S(2)}) collective-permute-start(bf16[48,2560]{1,0:T(8,128)(2,1)S(1)} %collective-permute-done.14.refs_9_), channel_id=1, source_target_pairs={{0,1},{1,0},{2,3},{3,2},{4,5},{5,4},{6,7},{7,6},{8,9},{9,8},{10,11... | collective-permute-start | bytes 737288 | tf_op jit(solution)/shard_map/ppermute | solution.py:374
  72.0 2.2 %collective-permute-start.19 = (bf16[48,2560]{1,0:T(8,128)(2,1)S(1)}, bf16[48,2560]{1,0:T(8,128)(2,1)S(1)}, u32[]{:S(2)}, u32[]{:S(2)}) collective-permute-start(bf16[48,2560]{1,0:T(8,128)(2,1)S(1)} %collective-permute-done.15.refs_10_), channel_id=1, source_target_pairs={{0,1},{1,0},{2,3},{3,2},{4,5},{5,4},{6,7},{7,6},{8,9},{9,8},{10,11... | collective-permute-start | bytes 737288 | tf_op jit(solution)/shard_map/ppermute | solution.py:374
  72.1 2.5 %collective-permute-start.20 = (bf16[48,2560]{1,0:T(8,128)(2,1)S(1)}, bf16[48,2560]{1,0:T(8,128)(2,1)S(1)}, u32[]{:S(2)}, u32[]{:S(2)}) collective-permute-start(bf16[48,2560]{1,0:T(8,128)(2,1)S(1)} %collective-permute-done.16.refs_11_), channel_id=1, source_target_pairs={{0,1},{1,0},{2,3},{3,2},{4,5},{5,4},{6,7},{7,6},{8,9},{9,8},{10,11... | collective-permute-start | bytes 737288 | tf_op jit(solution)/shard_map/ppermute | solution.py:374
  73.9 1.3 %copy-start.17 = (bf16[48,2560]{1,0:T(8,128)(2,1)}, bf16[48,2560]{1,0:T(8,128)(2,1)S(1)}, u32[]{:S(2)}) copy-start(bf16[48,2560]{1,0:T(8,128)(2,1)S(1)} %collective-permute-done.18.refs_13_) | copy-start | bytes 737284
  74.2 1.0 copy-start.18
  74.6 0.7 copy-start.19
  74.6 0.9 copy-start.10
  74.6 20.4 %collective-permute-start.21 = (bf16[2,192,1792]{2,1,0:T(8,128)(2,1)}, bf16[2,192,1792]{2,1,0:T(8,128)(2,1)S(1)}, u32[]{:S(2)}, u32[]{:S(2)}) collective-permute-start(bf16[2,192,1792]{2,1,0:T(8,128)(2,1)} %get-tuple-element.106), channel_id=1, source_target_pairs={{0,1},{1,0},{2,3},{3,2},{4,5},{5,4},{6,7},{7,6},{8,9},{9,8},{10,11... | collective-permute-start | bytes 4128776 | tf_op jit(solution)/shard_map/ppermute | solution.py:374
  74.7 20.3 %collective-permute-start.22 = (bf16[2,192,1792]{2,1,0:T(8,128)(2,1)}, bf16[2,192,1792]{2,1,0:T(8,128)(2,1)S(1)}, u32[]{:S(2)}, u32[]{:S(2)}) collective-permute-start(bf16[2,192,1792]{2,1,0:T(8,128)(2,1)} %get-tuple-element.107), channel_id=1, source_target_pairs={{0,1},{1,0},{2,3},{3,2},{4,5},{5,4},{6,7},{7,6},{8,9},{9,8},{10,11... | collective-permute-start | bytes 4128776 | tf_op jit(solution)/shard_map/ppermute | solution.py:374
  95.0 1.1 %copy-start.5 = (bf16[2,192,1792]{2,1,0:T(8,128)(2,1)}, bf16[2,192,1792]{2,1,0:T(8,128)(2,1)S(1)}, u32[]{:S(2)}) copy-start(bf16[2,192,1792]{2,1,0:T(8,128)(2,1)S(1)} %collective-permute-done.21.gate) | copy-start | bytes 4128772
  95.1 1.5 %copy-start.6 = (bf16[2,192,1792]{2,1,0:T(8,128)(2,1)}, bf16[2,192,1792]{2,1,0:T(8,128)(2,1)S(1)}, u32[]{:S(2)}) copy-start(bf16[2,192,1792]{2,1,0:T(8,128)(2,1)S(1)} %collective-permute-done.22.up) | copy-start | bytes 4128772

commit v3 on v2

--- a/solution.py
+++ b/solution.py
@@ -149,31 +149,6 @@
         cost_estimate=pl.CostEstimate(flops=1000, bytes_accessed=1000, transcendentals=0),
         name="assemble",
     )(at, *slots)
-
-
-def complete_kernel(at, slot, earlier, whole):
-    whole[...] = slot[...]
-
-
-def complete(at, slot, whole):
-    piece, width = slot.shape[0], whole.shape[1]
-    return pl.pallas_call(
-        complete_kernel,
-        grid_spec=pltpu.PrefetchScalarGridSpec(
-            num_scalar_prefetch=1,
-            grid=(1,),
-            in_specs=[
-                pl.BlockSpec((piece, width), lambda i, at: (0, 0)),
-                pl.BlockSpec(memory_space=pl.ANY),
-            ],
-            out_specs=pl.BlockSpec((piece, width), lambda i, at: (lax.rem(at[2] + 1, 4), 0)),
-        ),
-        out_shape=jax.ShapeDtypeStruct(whole.shape, jnp.bfloat16),
-        input_output_aliases={2: 0},
-        compiler_params=pltpu.CompilerParams(vmem_limit_bytes=VMEM_BYTES),
-        cost_estimate=pl.CostEstimate(flops=1000, bytes_accessed=1000, transcendentals=0),
-        name="complete",
-    )(at, slot, whole)
 
 
 def share_kernel(at, gate, up, gate_out, up_out):
@@ -333,30 +308,6 @@
     )(at, norm, *hidden, rows, rows, *low, *high, *own_new)
 
 
-def place_kernel(at, gate, up, earlier_gate, earlier_up, gate_out, up_out):
-    gate_out[...] = gate[...]
-    up_out[...] = up[...]
-
-
-def place_pair(at, news, wholes):
-    count, block = news[0].shape[1:]
-    return pl.pallas_call(
-        place_kernel,
-        grid_spec=pltpu.PrefetchScalarGridSpec(
-            num_scalar_prefetch=1,
-            grid=(2,),
-            in_specs=[pl.BlockSpec((None, count, block), lambda n, at: (n, 0, 0))] * 2
-            + [pl.BlockSpec(memory_space=pl.ANY)] * 2,
-            out_specs=[pl.BlockSpec((count, block), lambda n, at: (0, at[5 + n]))] * 2,
-        ),
-        out_shape=[jax.ShapeDtypeStruct(whole.shape, whole.dtype) for whole in wholes],
-        input_output_aliases={3: 0, 4: 1},
-        compiler_params=pltpu.CompilerParams(vmem_limit_bytes=VMEM_BYTES),
-        cost_estimate=pl.CostEstimate(flops=1000, bytes_accessed=1000, transcendentals=0),
-        name="place_pair",
-    )(at, *news, *wholes)
-
-
 def paired(section_layers, grad_out, gate_act, up_act, down_weight):
     place, replica = lax.axis_index("tensor"), lax.axis_index("dp")
     chip, core = replica // 2, replica % 2
@@ -396,10 +347,9 @@
     far_own = to_across(far_own)
     pair_gate, pair_up, near[1] = lax.optimization_barrier((pair_gate, pair_up, near[1]))
     near_theirs = factors(at, pair_gate, pair_up, block, -2)
-    near_mine = factors(at, pair_gate, pair_up, block, -1)
-
-    slots[2], far_near, gate, section_layers, _ = lax.optimization_barrier(
-        (slots[2], near_theirs[0], gate, section_layers, near_mine[0])
+
+    slots[2], far_near, gate, pair_gate, section_layers = lax.optimization_barrier(
+        (slots[2], near_theirs[0], gate, pair_gate, section_layers)
     )
     scale = section_scale(section_layers).reshape(1)
     norm = scale / jnp.sqrt(jnp.float32(rows * 4))
@@ -408,13 +358,16 @@
     cross_b = [to_pair(after(far_b0, slots[2]))]
     far_near = to_across(far_near)
     own_mine = factors(at, gate, up, block, 3)
+    near_mine = factors(at, pair_gate, pair_up, block, -1)
     part = assemble(at, slots[:3], split)
 
-    slots[3], near[2], cross_b[0], far_own, part, scale, norm, _ = lax.optimization_barrier(
-        (slots[3], near[2], cross_b[0], far_own, part, scale, norm, own_mine[0])
+    slots[3], near[2], cross_b[0], far_own, part, scale, norm, _, _ = lax.optimization_barrier(
+        (slots[3], near[2], cross_b[0], far_own, part, scale, norm, own_mine[0], near_mine[0])
     )
     near.append(to_pair(slots[3]))
-    far_a = to_across(complete(at, slots[3], part))
+    piece = slots[3].shape[0]
+    part = lax.dynamic_update_slice(part, slots[3][:, :split], (lax.rem(place + 1, 4) * piece, 0))
+    far_a = to_across(part)
     far_b = [far_b0] + [around(after(far_b0, slots[3]), places) for places in (1, 2, 3)]
 
     own_gate, own_up, near_gate, near_up, rows_here = hidden_grad(
@@ -435,7 +388,9 @@
     grad_gate, grad_up, grad_down_w = weight_grad(
         at, norm, hidden, rows_here, [far_a, cross_a], [*far_b, *cross_b], [own_gate, own_up]
     )
-    grad_gate, grad_up = place_pair(at, from_pair, [grad_gate, grad_up])
+    for i, owner in enumerate((pair_mine, pair_theirs)):
+        grad_gate = lax.dynamic_update_slice(grad_gate, from_pair[0][i], (0, owner * block))
+        grad_up = lax.dynamic_update_slice(grad_up, from_pair[1][i], (0, owner * block))
     return (grad_gate[None, None], grad_up[None, None], grad_down_w[None])
 
 

time: 101 us -> 98.8 us (0.978)
  Pallas kernels: 67.1 us -> 61.1 us
  local copies, waits for them, and re-layouts: 5.3 us -> 9.36 us
    pallas_call x2 -> x0, Pallas kernels: 5.85 us -> none  [the longest x1 3.61 us: place_pair(): pl.pallas_call(place_kernel, grid_spec=pltpu.PrefetchScalarGridSpec(num_s...]
    dynamic_update_slice x0 -> x5, local copies, waits for them, and re-layouts: none -> 3.59 us  [the longest x2 1.79 us: paired(): lax.dynamic_update_slice(grad_gate, from_pair[0][i], (0, owner * block))]
    ppermute x6, starting transfers between devices: 4.78 us -> 7.17 us  [around(): lax.ppermute(value, 'tensor', [(i, (i + places) % 4) for i in range(4)])]
    ppermute x4, starting transfers between devices: 6.08 us -> 4.62 us  [to_across(): return lax.ppermute(value, 'dp', across)]
    unnamed x42 -> x40, local copies, waits for them, and re-layouts: 3.7 us -> 4.19 us
  transfers between devices with their start and end apart: 23 -> 23, of which waited for: 7 -> 7; matrix products, arithmetic and copies ran while one was open for 2% -> 4% of each run, Pallas kernels for 63% -> 62%
where the time goes in v3:
time: 98.8 us; the launch traced here: 98.4 us
  Pallas kernels  61.1 us (62%)
  starting transfers between devices  15 us (15%)
  waiting for transfers between devices  9.91 us (10%)
  local copies, waits for them, and re-layouts  9.36 us (9%)
  between operations  2.32 us (2%)
    pallas_call x1, Pallas kernels, hidden_grad(): pl.pallas_call(hidden_grad_kernel, grid_spec=pltpu.PrefetchScalarGridSpec...  21.5 us
    pallas_call x1, Pallas kernels, weight_grad(): pl.pallas_call(functools.partial(weight_grad_kernel, low_steps), grid_spe...  19.5 us
    pallas_call x4, Pallas kernels, factors(): pl.pallas_call(factors_kernel, grid_spec=pltpu.PrefetchScalarGridSpec(num...  13.8 us
    ppermute x6, starting transfers between devices, around(): lax.ppermute(value, 'tensor', [(i, (i + places) % 4) for i in range(4)])  7.17 us
    ppermute x13, waiting for transfers between devices, to_pair(): return lax.ppermute(value, 'dp', pair)  5.06 us
    ppermute x6, waiting for transfers between devices, around(): lax.ppermute(value, 'tensor', [(i, (i + places) % 4) for i in range(4)])  4.84 us
    ppermute x4, starting transfers between devices, to_across(): return lax.ppermute(value, 'dp', across)  4.62 us
    unnamed x40, local copies, waits for them, and re-layouts  4.19 us
  transfers between devices with their start and end apart: 23, of which 7 were waited for; matrix products, arithmetic and copies ran while one was open for 4% of the time, Pallas kernels for 62%

profile of v3, /device:TPU:0, one launch (start us, length us, event | category | flops | bytes accessed | tf_op | source)
XLA Modules:
  0.0 98.4 jit_solution(6148244018431916195)
XLA Ops:
  0.6 0.5 collective-permute-start.2
  1.1 2.6 %collective-permute-start = (bf16[48,4096]{1,0:T(8,128)(2,1)}, bf16[48,4096]{1,0:T(8,128)(2,1)S(1)}, u32[]{:S(2)}, u32[]{:S(2)}) collective-permute-start(bf16[48,4096]{1,0:T(8,128)(2,1)} %bitcast.39), channel_id=1, source_target_pairs={{0,4},{4,8},{8,12},{12,0},{1,5},{5,9},{9,13},{13,1},{2,6},{6,10},{... | collective-permute-start | bytes 1179656 | tf_op jit(solution)/shard_map/ppermute | solution.py:331
  3.8 1.0 %slice.24 = bf16[48,2560]{1,0:T(8,128)(2,1)S(1)} slice(bf16[48,4096]{1,0:T(8,128)(2,1)} %bitcast.40), slice={[0:48], [1536:4096]} | slice | bytes 491520 | tf_op jit(solution)/shard_map/slice | solution.py:336
  4.8 1.6 %collective-permute-start.1 = (bf16[48,2560]{1,0:T(8,128)(2,1)S(1)}, bf16[48,2560]{1,0:T(8,128)(2,1)}, u32[]{:S(2)}, u32[]{:S(2)}) collective-permute-start(bf16[48,2560]{1,0:T(8,128)(2,1)S(1)} %slice.24), channel_id=1, source_target_pairs={{0,2},{1,3},{2,0},{3,1},{4,6},{5,7},{6,4},{7,5},{8,10},{9,11},{10,... | collective-permute-start | bytes 737288 | tf_op jit(solution)/shard_map/ppermute | solution.py:328
  6.4 0.6 stack.31.at
  7.0 3.5 %factors.4 = (bf16[192,1792]{1,0:T(8,128)(2,1)}, bf16[192,1792]{1,0:T(8,128)(2,1)}, bf16[192,1792]{1,0:T(8,128)(2,1)}) custom-call(s32[7]{0:T(128)} %stack.31.at, bf16[192,7168]{1,0:T(8,128)(2,1)} %bitcast.32, bf16[192,7168]{1,0:T(8,128)(2,1)} %bitcast.35), custom_call_target="tpu_custom_call" | custom-call | flops 1000 | bytes 1000 | tf_op jit(solution)/shard_map/factors/pallas_call | solution.py:113
  10.5 3.6 %share.1 = (bf16[192,3584]{1,0:T(8,128)(2,1)}, bf16[192,3584]{1,0:T(8,128)(2,1)}) custom-call(s32[7]{0:T(128)} %stack.31.at, bf16[192,7168]{1,0:T(8,128)(2,1)} %bitcast.33, bf16[192,7168]{1,0:T(8,128)(2,1)} %bitcast.36), custom_call_target="tpu_custom_call" | custom-call | flops 1000 | bytes 1000 | tf_op jit(solution)/shard_map/share/pallas_call | solution.py:163
  14.1 1.6 %collective-permute-done.refs_1_ = bf16[48,4096]{1,0:T(8,128)(2,1)S(1)} collective-permute-done((bf16[48,4096]{1,0:T(8,128)(2,1)}, bf16[48,4096]{1,0:T(8,128)(2,1)S(1)}, u32[]{:S(2)}, u32[]{:S(2)}) %collective-permute-start) | collective-permute-done | bytes 393248 | tf_op jit(solution)/shard_map/ppermute | solution.py:331
  15.8 0.5 collective-permute-start.5
  16.3 0.1 collective-permute-start.6
  16.3 0.6 collective-permute-start.3
  17.0 0.9 collective-permute-start.10
  17.9 2.1 %collective-permute-done.6.refs_5_ = bf16[48,4096]{1,0:T(8,128)(2,1)S(1)} collective-permute-done((bf16[48,4096]{1,0:T(8,128)(2,1)S(1)}, bf16[48,4096]{1,0:T(8,128)(2,1)S(1)}, u32[]{:S(2)}, u32[]{:S(2)}) %collective-permute-start.6) | collective-permute-done | bytes 393248 | tf_op jit(solution)/shard_map/ppermute | solution.py:325
  20.0 0.7 copy-done.9
  20.8 0.9 collective-permute-done.5.up
  21.6 0.2 copy-done
  21.8 1.1 %copy-done.1 = bf16[192,3584]{1,0:T(8,128)(2,1)} copy-done((bf16[192,3584]{1,0:T(8,128)(2,1)}, bf16[192,3584]{1,0:T(8,128)(2,1)S(1)}, u32[]{:S(2)}) %copy-start.1) | copy-done | bytes 1376280
  22.9 3.5 %factors.5 = (bf16[192,1792]{1,0:T(8,128)(2,1)}, bf16[192,1792]{1,0:T(8,128)(2,1)}, bf16[192,1792]{1,0:T(8,128)(2,1)}) custom-call(s32[7]{0:T(128)} %stack.31.at, bf16[192,3584]{1,0:T(8,128)(2,1)} %copy-done, bf16[192,3584]{1,0:T(8,128)(2,1)} %copy-done.1), custom_call_target="tpu_custom_call" | custom-call | flops 1000 | bytes 1000 | tf_op jit(solution)/shard_map/factors/pallas_call | solution.py:113
  26.4 3.2 %collective-permute-done.3.refs_2_ = bf16[48,4096]{1,0:T(8,128)(2,1)S(1)} collective-permute-done((bf16[48,4096]{1,0:T(8,128)(2,1)S(1)}, bf16[48,4096]{1,0:T(8,128)(2,1)S(1)}, u32[]{:S(2)}, u32[]{:S(2)}) %collective-permute-start.3) | collective-permute-done | bytes 393248 | tf_op jit(solution)/shard_map/ppermute | solution.py:331
  29.6 0.5 collective-permute-start.9
  30.1 0.2 copy-done.3
  30.3 2.6 %assemble.1 = bf16[192,1536]{1,0:T(8,128)(2,1)} custom-call(s32[7]{0:T(128)} %stack.31.at, bf16[48,4096]{1,0:T(8,128)(2,1)} %bitcast.41, bf16[48,4096]{1,0:T(8,128)(2,1)} %copy-done.2, bf16[48,4096]{1,0:T(8,128)(2,1)} %copy-done.3), custom_call_target="tpu_custom_call" | custom-call | flops 1000 | bytes 1000 | tf_op jit(solution)/shard_map/assemble/pallas_call | solution.py:139
  32.9 3.4 %factors.7 = (bf16[192,1792]{1,0:T(8,128)(2,1)}, bf16[192,1792]{1,0:T(8,128)(2,1)}, bf16[192,1792]{1,0:T(8,128)(2,1)}) custom-call(s32[7]{0:T(128)} %stack.31.at, bf16[192,3584]{1,0:T(8,128)(2,1)} %copy-done, bf16[192,3584]{1,0:T(8,128)(2,1)} %copy-done.1), custom_call_target="tpu_custom_call" | custom-call | flops 1000 | bytes 1000 | tf_op jit(solution)/shard_map/factors/pallas_call | solution.py:113
  36.3 1.6 %collective-permute-start.12 = (bf16[192,1792]{1,0:T(8,128)(2,1)}, bf16[192,1792]{1,0:T(8,128)(2,1)S(1)}, u32[]{:S(2)}, u32[]{:S(2)}) collective-permute-start(bf16[192,1792]{1,0:T(8,128)(2,1)} %get-tuple-element.98), channel_id=1, source_target_pairs={{0,2},{1,3},{2,0},{3,1},{4,6},{5,7},{6,4},{7,5},{8,10},{9,11},{10,... | collective-permute-start | bytes 2064392 | tf_op jit(solution)/shard_map/ppermute | solution.py:328
  37.9 3.4 %factors.6 = (bf16[192,1792]{1,0:T(8,128)(2,1)}, bf16[192,1792]{1,0:T(8,128)(2,1)}, bf16[192,1792]{1,0:T(8,128)(2,1)}) custom-call(s32[7]{0:T(128)} %stack.31.at, bf16[192,7168]{1,0:T(8,128)(2,1)} %bitcast.34, bf16[192,7168]{1,0:T(8,128)(2,1)} %bitcast.37), custom_call_target="tpu_custom_call" | custom-call | flops 1000 | bytes 1000 | tf_op jit(solution)/shard_map/factors/pallas_call | solution.py:113
  41.4 0.7 fusion.5
  43.6 0.7 copy-done.12
  44.3 0.6 collective-permute-start.13
  44.9 3.3 %collective-permute-start.16 = (bf16[48,2560]{1,0:T(8,128)(2,1)}, bf16[48,2560]{1,0:T(8,128)(2,1)S(1)}, u32[]{:S(2)}, u32[]{:S(2)}) collective-permute-start(bf16[48,2560]{1,0:T(8,128)(2,1)} %collective-permute-done.1.refs_8_), channel_id=1, source_target_pairs={{0,12},{4,0},{8,4},{12,8},{1,13},{5,1},{9,5},{13,9},{2,14},{6,2},{... | collective-permute-start | bytes 737288 | tf_op jit(solution)/shard_map/ppermute | solution.py:331
  48.2 0.6 collective-permute-start.14
  48.8 0.2 copy-done.11
  49.0 21.5 %hidden_grad.1 = (bf16[2,192,1792]{2,1,0:T(8,128)(2,1)}, bf16[2,192,1792]{2,1,0:T(8,128)(2,1)}, bf16[2,192,1792]{2,1,0:T(8,128)(2,1)}, bf16[2,192,1792]{2,1,0:T(8,128)(2,1)}, bf16[384,4096]{1,0:T(8,128)(2,1)}) custom-call(s32[7]{0:T(128)} %stack.31.at, f32[1]{0:T(128)} %bitcast.10.scale, bf16[48,4096]{1,0:T(8,128)(2,1)} %bitcast.42, ...), custom_call_target="tpu_custom_call" | custom-call | flops 1000 | bytes 1000 | tf_op jit(solution)/shard_map/hidden_grad/pallas_call | solution.py:217
  70.6 0.1 collective-permute-start.17
  70.7 0.5 collective-permute-start.18
  71.2 0.1 collective-permute-start.19
  71.3 0.4 collective-permute-start.20
  71.7 1.3 %collective-permute-done.18.refs_13_ = bf16[48,2560]{1,0:T(8,128)(2,1)S(1)} collective-permute-done((bf16[48,2560]{1,0:T(8,128)(2,1)S(1)}, bf16[48,2560]{1,0:T(8,128)(2,1)S(1)}, u32[]{:S(2)}, u32[]{:S(2)}) %collective-permute-start.18) | collective-permute-done | bytes 245792 | tf_op jit(solution)/shard_map/ppermute | solution.py:325
  73.0 0.3 collective-permute-done.19.refs_14_
  73.4 0.3 collective-permute-done.20.refs_15_
  73.7 0.3 copy-done.17
  74.1 0.7 copy-done.18
  74.8 0.2 collective-permute-start.21
  75.0 0.4 collective-permute-start.22
  75.3 19.5 %weight_grad.1 = (bf16[192,7168]{1,0:T(8,128)(2,1)}, bf16[192,7168]{1,0:T(8,128)(2,1)}, bf16[1792,4096]{1,0:T(8,128)(2,1)}) custom-call(s32[7]{0:T(128)} %stack.31.at, f32[1]{0:T(128)S(6)} %div.18.norm, bf16[192,1792]{1,0:T(8,128)(2,1)} %get-tuple-element.78.refs_0_, bf16[192,1792]{1,0:T(8,128)(2,1)} %get-tuple-element.80.refs_1_, ...), custom_call_target="tpu_custom_call" | custom-call | flops 1000 | bytes 1000 | tf_op jit(solution)/shard_map/weight_grad/pallas_call | solution.py:291
  94.9 0.9 fusion.3
  95.8 0.9 fusion.2
  96.6 0.9 fusion.1
  97.5 0.9 fusion
  (54 shorter events, 0.1 us)
Async XLA Ops:
  0.6 13.5 %collective-permute-start.2 = (bf16[48,4096]{1,0:T(8,128)(2,1)}, bf16[48,4096]{1,0:T(8,128)(2,1)S(1)}, u32[]{:S(2)}, u32[]{:S(2)}) collective-permute-start(bf16[48,4096]{1,0:T(8,128)(2,1)} %bitcast.38), channel_id=1, source_target_pairs={{0,1},{1,0},{2,3},{3,2},{4,5},{5,4},{6,7},{7,6},{8,9},{9,8},{10,11... | collective-permute-start | bytes 1179656 | tf_op jit(solution)/shard_map/ppermute | solution.py:325
  1.1 14.6 %collective-permute-start = (bf16[48,4096]{1,0:T(8,128)(2,1)}, bf16[48,4096]{1,0:T(8,128)(2,1)S(1)}, u32[]{:S(2)}, u32[]{:S(2)}) collective-permute-start(bf16[48,4096]{1,0:T(8,128)(2,1)} %bitcast.39), channel_id=1, source_target_pairs={{0,4},{4,8},{8,12},{12,0},{1,5},{5,9},{9,13},{13,1},{2,6},{6,10},{... | collective-permute-start | bytes 1179656 | tf_op jit(solution)/shard_map/ppermute | solution.py:331
  4.8 9.3 %collective-permute-start.1 = (bf16[48,2560]{1,0:T(8,128)(2,1)S(1)}, bf16[48,2560]{1,0:T(8,128)(2,1)}, u32[]{:S(2)}, u32[]{:S(2)}) collective-permute-start(bf16[48,2560]{1,0:T(8,128)(2,1)S(1)} %slice.24), channel_id=1, source_target_pairs={{0,2},{1,3},{2,0},{3,1},{4,6},{5,7},{6,4},{7,5},{8,10},{9,11},{10,... | collective-permute-start | bytes 737288 | tf_op jit(solution)/shard_map/ppermute | solution.py:328
  14.1 1.6 %copy-start.8 = (bf16[48,4096]{1,0:T(8,128)(2,1)}, bf16[48,4096]{1,0:T(8,128)(2,1)S(1)}, u32[]{:S(2)}) copy-start(bf16[48,4096]{1,0:T(8,128)(2,1)S(1)} %collective-permute-done.2.refs_4_) | copy-start | bytes 1179652
  15.7 14.4 %copy-start.2 = (bf16[48,4096]{1,0:T(8,128)(2,1)}, bf16[48,4096]{1,0:T(8,128)(2,1)S(1)}, u32[]{:S(2)}) copy-start(bf16[48,4096]{1,0:T(8,128)(2,1)S(1)} %collective-permute-done.refs_1_) | copy-start | bytes 1179652
  15.7 4.3 %collective-permute-start.4 = (bf16[192,3584]{1,0:T(8,128)(2,1)}, bf16[192,3584]{1,0:T(8,128)(2,1)S(1)}, u32[]{:S(2)}, u32[]{:S(2)}) collective-permute-start(bf16[192,3584]{1,0:T(8,128)(2,1)} %get-tuple-element.67), channel_id=1, source_target_pairs={{0,1},{1,0},{2,3},{3,2},{4,5},{5,4},{6,7},{7,6},{8,9},{9,8},{10,11... | collective-permute-start | bytes 4128776 | tf_op jit(solution)/shard_map/ppermute | solution.py:325
  15.8 5.9 %collective-permute-start.5 = (bf16[192,3584]{1,0:T(8,128)(2,1)}, bf16[192,3584]{1,0:T(8,128)(2,1)S(1)}, u32[]{:S(2)}, u32[]{:S(2)}) collective-permute-start(bf16[192,3584]{1,0:T(8,128)(2,1)} %get-tuple-element.68), channel_id=1, source_target_pairs={{0,1},{1,0},{2,3},{3,2},{4,5},{5,4},{6,7},{7,6},{8,9},{9,8},{10,11... | collective-permute-start | bytes 4128776 | tf_op jit(solution)/shard_map/ppermute | solution.py:325
  16.3 3.7 %collective-permute-start.6 = (bf16[48,4096]{1,0:T(8,128)(2,1)S(1)}, bf16[48,4096]{1,0:T(8,128)(2,1)S(1)}, u32[]{:S(2)}, u32[]{:S(2)}) collective-permute-start(bf16[48,4096]{1,0:T(8,128)(2,1)S(1)} %collective-permute-done.refs_1_), channel_id=1, source_target_pairs={{0,1},{1,0},{2,3},{3,2},{4,5},{5,4},{6,7},{7,6},{8,9},{9,8},{10,11... | collective-permute-start | bytes 1179656 | tf_op jit(solution)/shard_map/ppermute | solution.py:325
  16.3 13.3 %collective-permute-start.3 = (bf16[48,4096]{1,0:T(8,128)(2,1)S(1)}, bf16[48,4096]{1,0:T(8,128)(2,1)S(1)}, u32[]{:S(2)}, u32[]{:S(2)}) collective-permute-start(bf16[48,4096]{1,0:T(8,128)(2,1)S(1)} %collective-permute-done.refs_1_), channel_id=1, source_target_pairs={{0,4},{4,8},{8,12},{12,0},{1,5},{5,9},{9,13},{13,1},{2,6},{6,10},{... | collective-permute-start | bytes 1179656 | tf_op jit(solution)/shard_map/ppermute | solution.py:331
  17.0 26.6 %collective-permute-start.10 = (bf16[192,1792]{1,0:T(8,128)(2,1)}, bf16[192,1792]{1,0:T(8,128)(2,1)}, u32[]{:S(2)}, u32[]{:S(2)}) collective-permute-start(bf16[192,1792]{1,0:T(8,128)(2,1)} %get-tuple-element.75), channel_id=1, source_target_pairs={{0,2},{1,3},{2,0},{3,1},{4,6},{5,7},{6,4},{7,5},{8,10},{9,11},{10,... | collective-permute-start | bytes 2064392 | tf_op jit(solution)/shard_map/ppermute | solution.py:328
  20.0 0.8 copy-start.9
  20.8 1.1 %copy-start = (bf16[192,3584]{1,0:T(8,128)(2,1)}, bf16[192,3584]{1,0:T(8,128)(2,1)S(1)}, u32[]{:S(2)}) copy-start(bf16[192,3584]{1,0:T(8,128)(2,1)S(1)} %collective-permute-done.4.gate) | copy-start | bytes 4128772
  21.8 1.1 %copy-start.1 = (bf16[192,3584]{1,0:T(8,128)(2,1)}, bf16[192,3584]{1,0:T(8,128)(2,1)S(1)}, u32[]{:S(2)}) copy-start(bf16[192,3584]{1,0:T(8,128)(2,1)S(1)} %collective-permute-done.5.up) | copy-start | bytes 4128772
  29.6 0.7 copy-start.3
  29.6 14.0 %collective-permute-start.8 = (bf16[48,4096]{1,0:T(8,128)(2,1)S(1)}, bf16[48,4096]{1,0:T(8,128)(2,1)S(1)}, u32[]{:S(2)}, u32[]{:S(2)}) collective-permute-start(bf16[48,4096]{1,0:T(8,128)(2,1)S(1)} %collective-permute-done.3.refs_2_), channel_id=1, source_target_pairs={{0,1},{1,0},{2,3},{3,2},{4,5},{5,4},{6,7},{7,6},{8,9},{9,8},{10,11... | collective-permute-start | bytes 1179656 | tf_op jit(solution)/shard_map/ppermute | solution.py:325
  29.6 14.0 %collective-permute-start.7 = (bf16[48,4096]{1,0:T(8,128)(2,1)S(1)}, bf16[48,4096]{1,0:T(8,128)(2,1)S(1)}, u32[]{:S(2)}, u32[]{:S(2)}) collective-permute-start(bf16[48,4096]{1,0:T(8,128)(2,1)S(1)} %collective-permute-done.3.refs_2_), channel_id=1, source_target_pairs={{0,4},{4,8},{8,12},{12,0},{1,5},{5,9},{9,13},{13,1},{2,6},{6,10},{... | collective-permute-start | bytes 1179656 | tf_op jit(solution)/shard_map/ppermute | solution.py:331
  29.6 14.0 %collective-permute-start.9 = (bf16[48,2560]{1,0:T(8,128)(2,1)}, bf16[48,2560]{1,0:T(8,128)(2,1)S(1)}, u32[]{:S(2)}, u32[]{:S(2)}) collective-permute-start(bf16[48,2560]{1,0:T(8,128)(2,1)} %collective-permute-done.1.refs_8_), channel_id=1, source_target_pairs={{0,1},{1,0},{2,3},{3,2},{4,5},{5,4},{6,7},{7,6},{8,9},{9,8},{10,11... | collective-permute-start | bytes 737288 | tf_op jit(solution)/shard_map/ppermute | solution.py:325
  36.3 5.0 %copy-start.19 = (s32[2]{0:T(128)S(1)}, s32[2]{0:T(128)}, u32[]{:S(2)}) copy-start(s32[2]{0:T(128)} %param.5) | copy-start | bytes 28
  36.3 7.9 %copy-start.6 = (bf16[192,1536]{1,0:T(8,128)(2,1)S(1)}, bf16[192,1536]{1,0:T(8,128)(2,1)}, u32[]{:S(2)}) copy-start(bf16[192,1536]{1,0:T(8,128)(2,1)} %assemble.1) | copy-start | bytes 1769476
  36.3 34.2 %collective-permute-start.12 = (bf16[192,1792]{1,0:T(8,128)(2,1)}, bf16[192,1792]{1,0:T(8,128)(2,1)S(1)}, u32[]{:S(2)}, u32[]{:S(2)}) collective-permute-start(bf16[192,1792]{1,0:T(8,128)(2,1)} %get-tuple-element.98), channel_id=1, source_target_pairs={{0,2},{1,3},{2,0},{3,1},{4,6},{5,7},{6,4},{7,5},{8,10},{9,11},{10,... | collective-permute-start | bytes 2064392 | tf_op jit(solution)/shard_map/ppermute | solution.py:328
  43.6 0.7 copy-start.12
  43.6 5.2 %copy-start.10 = (bf16[48,4096]{1,0:T(8,128)(2,1)}, bf16[48,4096]{1,0:T(8,128)(2,1)S(1)}, u32[]{:S(2)}) copy-start(bf16[48,4096]{1,0:T(8,128)(2,1)S(1)} %collective-permute-done.8.refs_6_) | copy-start | bytes 1179652
  43.6 5.2 %copy-start.4 = (bf16[48,4096]{1,0:T(8,128)(2,1)}, bf16[48,4096]{1,0:T(8,128)(2,1)S(1)}, u32[]{:S(2)}) copy-start(bf16[48,4096]{1,0:T(8,128)(2,1)S(1)} %collective-permute-done.7.refs_3_) | copy-start | bytes 1179652
  44.3 3.9 %collective-permute-start.11 = (bf16[48,4096]{1,0:T(8,128)(2,1)S(1)}, bf16[48,4096]{1,0:T(8,128)(2,1)S(1)}, u32[]{:S(2)}, u32[]{:S(2)}) collective-permute-start(bf16[48,4096]{1,0:T(8,128)(2,1)S(1)} %collective-permute-done.7.refs_3_), channel_id=1, source_target_pairs={{0,1},{1,0},{2,3},{3,2},{4,5},{5,4},{6,7},{7,6},{8,9},{9,8},{10,11... | collective-permute-start | bytes 1179656 | tf_op jit(solution)/shard_map/ppermute | solution.py:325
  44.3 26.3 %collective-permute-start.13 = (bf16[192,1536]{1,0:T(8,128)(2,1)S(1)}, bf16[192,1536]{1,0:T(8,128)(2,1)S(1)}, u32[]{:S(2)}, u32[]{:S(2)}) collective-permute-start(bf16[192,1536]{1,0:T(8,128)(2,1)S(1)} %slice_dynamic-update-slice_fusion), channel_id=1, source_target_pairs={{0,2},{1,3},{2,0},{3,1},{4,6},{5,7},{6,4},{7,5},{8,10},{9,11},{10,... | collective-permute-start | bytes 1769480 | tf_op jit(solution)/shard_map/ppermute | solution.py:328
  44.9 25.6 %collective-permute-start.16 = (bf16[48,2560]{1,0:T(8,128)(2,1)}, bf16[48,2560]{1,0:T(8,128)(2,1)S(1)}, u32[]{:S(2)}, u32[]{:S(2)}) collective-permute-start(bf16[48,2560]{1,0:T(8,128)(2,1)} %collective-permute-done.1.refs_8_), channel_id=1, source_target_pairs={{0,12},{4,0},{8,4},{12,8},{1,13},{5,1},{9,5},{13,9},{2,14},{6,2},{... | collective-permute-start | bytes 737288 | tf_op jit(solution)/shard_map/ppermute | solution.py:331
  48.2 22.3 %collective-permute-start.15 = (bf16[48,2560]{1,0:T(8,128)(2,1)}, bf16[48,2560]{1,0:T(8,128)(2,1)S(1)}, u32[]{:S(2)}, u32[]{:S(2)}) collective-permute-start(bf16[48,2560]{1,0:T(8,128)(2,1)} %collective-permute-done.1.refs_8_), channel_id=1, source_target_pairs={{0,8},{4,12},{8,0},{12,4},{1,9},{5,13},{9,1},{13,5},{2,10},{6,14},... | collective-permute-start | bytes 737288 | tf_op jit(solution)/shard_map/ppermute | solution.py:331
  48.2 0.8 copy-start.11
  48.2 22.3 %collective-permute-start.14 = (bf16[48,2560]{1,0:T(8,128)(2,1)}, bf16[48,2560]{1,0:T(8,128)(2,1)S(1)}, u32[]{:S(2)}, u32[]{:S(2)}) collective-permute-start(bf16[48,2560]{1,0:T(8,128)(2,1)} %collective-permute-done.1.refs_8_), channel_id=1, source_target_pairs={{0,4},{4,8},{8,12},{12,0},{1,5},{5,9},{9,13},{13,1},{2,6},{6,10},{... | collective-permute-start | bytes 737288 | tf_op jit(solution)/shard_map/ppermute | solution.py:331
  70.5 3.2 %copy-start.13 = (bf16[48,2560]{1,0:T(8,128)(2,1)}, bf16[48,2560]{1,0:T(8,128)(2,1)S(1)}, u32[]{:S(2)}) copy-start(bf16[48,2560]{1,0:T(8,128)(2,1)S(1)} %collective-permute-done.16.refs_11_) | copy-start | bytes 737284
  70.5 4.4 %copy-start.14 = (bf16[48,2560]{1,0:T(8,128)(2,1)}, bf16[48,2560]{1,0:T(8,128)(2,1)S(1)}, u32[]{:S(2)}) copy-start(bf16[48,2560]{1,0:T(8,128)(2,1)S(1)} %collective-permute-done.15.refs_10_) | copy-start | bytes 737284
  70.5 4.4 %copy-start.15 = (bf16[48,2560]{1,0:T(8,128)(2,1)}, bf16[48,2560]{1,0:T(8,128)(2,1)S(1)}, u32[]{:S(2)}) copy-start(bf16[48,2560]{1,0:T(8,128)(2,1)S(1)} %collective-permute-done.14.refs_9_) | copy-start | bytes 737284
  70.6 4.2 %copy-start.5 = (bf16[192,1792]{1,0:T(8,128)(2,1)}, bf16[192,1792]{1,0:T(8,128)(2,1)S(1)}, u32[]{:S(2)}) copy-start(bf16[192,1792]{1,0:T(8,128)(2,1)S(1)} %collective-permute-done.12.refs_3_) | copy-start | bytes 2064388
  70.6 4.7 %copy-start.7 = (bf16[192,1536]{1,0:T(8,128)(2,1)}, bf16[192,1536]{1,0:T(8,128)(2,1)S(1)}, u32[]{:S(2)}) copy-start(bf16[192,1536]{1,0:T(8,128)(2,1)S(1)} %collective-permute-done.13.refs_6_) | copy-start | bytes 1769476
  70.6 4.1 %collective-permute-start.17 = (bf16[192,1536]{1,0:T(8,128)(2,1)S(1)}, bf16[192,1536]{1,0:T(8,128)(2,1)}, u32[]{:S(2)}, u32[]{:S(2)}) collective-permute-start(bf16[192,1536]{1,0:T(8,128)(2,1)S(1)} %collective-permute-done.13.refs_6_), channel_id=1, source_target_pairs={{0,1},{1,0},{2,3},{3,2},{4,5},{5,4},{6,7},{7,6},{8,9},{9,8},{10,11... | collective-permute-start | bytes 1769480 | tf_op jit(solution)/shard_map/ppermute | solution.py:325
  70.7 2.3 %collective-permute-start.18 = (bf16[48,2560]{1,0:T(8,128)(2,1)S(1)}, bf16[48,2560]{1,0:T(8,128)(2,1)S(1)}, u32[]{:S(2)}, u32[]{:S(2)}) collective-permute-start(bf16[48,2560]{1,0:T(8,128)(2,1)S(1)} %collective-permute-done.14.refs_9_), channel_id=1, source_target_pairs={{0,1},{1,0},{2,3},{3,2},{4,5},{5,4},{6,7},{7,6},{8,9},{9,8},{10,11... | collective-permute-start | bytes 737288 | tf_op jit(solution)/shard_map/ppermute | solution.py:325
  71.2 2.2 %collective-permute-start.19 = (bf16[48,2560]{1,0:T(8,128)(2,1)S(1)}, bf16[48,2560]{1,0:T(8,128)(2,1)S(1)}, u32[]{:S(2)}, u32[]{:S(2)}) collective-permute-start(bf16[48,2560]{1,0:T(8,128)(2,1)S(1)} %collective-permute-done.15.refs_10_), channel_id=1, source_target_pairs={{0,1},{1,0},{2,3},{3,2},{4,5},{5,4},{6,7},{7,6},{8,9},{9,8},{10,11... | collective-permute-start | bytes 737288 | tf_op jit(solution)/shard_map/ppermute | solution.py:325
  71.3 2.5 %collective-permute-start.20 = (bf16[48,2560]{1,0:T(8,128)(2,1)S(1)}, bf16[48,2560]{1,0:T(8,128)(2,1)S(1)}, u32[]{:S(2)}, u32[]{:S(2)}) collective-permute-start(bf16[48,2560]{1,0:T(8,128)(2,1)S(1)} %collective-permute-done.16.refs_11_), channel_id=1, source_target_pairs={{0,1},{1,0},{2,3},{3,2},{4,5},{5,4},{6,7},{7,6},{8,9},{9,8},{10,11... | collective-permute-start | bytes 737288 | tf_op jit(solution)/shard_map/ppermute | solution.py:325
  73.0 1.7 %copy-start.16 = (bf16[48,2560]{1,0:T(8,128)(2,1)}, bf16[48,2560]{1,0:T(8,128)(2,1)S(1)}, u32[]{:S(2)}) copy-start(bf16[48,2560]{1,0:T(8,128)(2,1)S(1)} %collective-permute-done.18.refs_13_) | copy-start | bytes 737284
  73.4 0.7 copy-start.17
  74.1 0.7 copy-start.18
  74.8 20.1 %collective-permute-start.21 = (bf16[2,192,1792]{2,1,0:T(8,128)(2,1)}, bf16[2,192,1792]{2,1,0:T(8,128)(2,1)S(1)}, u32[]{:S(2)}, u32[]{:S(2)}) collective-permute-start(bf16[2,192,1792]{2,1,0:T(8,128)(2,1)} %get-tuple-element.119), channel_id=1, source_target_pairs={{0,1},{1,0},{2,3},{3,2},{4,5},{5,4},{6,7},{7,6},{8,9},{9,8},{10,11... | collective-permute-start | bytes 4128776 | tf_op jit(solution)/shard_map/ppermute | solution.py:325
  75.0 21.7 %collective-permute-start.22 = (bf16[2,192,1792]{2,1,0:T(8,128)(2,1)}, bf16[2,192,1792]{2,1,0:T(8,128)(2,1)S(1)}, u32[]{:S(2)}, u32[]{:S(2)}) collective-permute-start(bf16[2,192,1792]{2,1,0:T(8,128)(2,1)} %get-tuple-element.121), channel_id=1, source_target_pairs={{0,1},{1,0},{2,3},{3,2},{4,5},{5,4},{6,7},{7,6},{8,9},{9,8},{10,11... | collective-permute-start | bytes 4128776 | tf_op jit(solution)/shard_map/ppermute | solution.py:325

commit v4 on v3

--- a/solution.py
+++ b/solution.py
@@ -179,7 +179,8 @@
     slots, weight = refs[:8], refs[8]
     own_mine, own_theirs, pair_mine, pair_theirs = refs[9:11], refs[11:13], refs[13:15], refs[15:17]
     own_out, pair_out = refs[17:19], refs[19:21]
-    rows, product = refs[21:]
+    rows_out, product, rows, sem = refs[21:]
+    copy_out = pltpu.make_async_copy(rows, rows_out, sem)
     chip, place = at[1], at[2]
     piece = slots[0].shape[0]
     count = 4 * piece
@@ -191,6 +192,7 @@
             rows[pl.ds(pl.multiple_of(block * piece, piece), piece), :] = slots[j][...]
             there = pl.ds(pl.multiple_of(count + block * piece, piece), piece)
             rows[there, :] = slots[4 + j][...]
+        copy_out.start()
 
     units = weight.shape[2]
     both = weight[...].reshape(2 * units, weight.shape[3])
@@ -205,6 +207,10 @@
             out[half] = (here[:count] * factor[...].astype(jnp.float32)).astype(jnp.bfloat16)
         for out, factor in zip(pair_out, pair):
             out[half] = (here[count:] * factor[...].astype(jnp.float32)).astype(jnp.bfloat16)
+
+    @pl.when(pl.program_id(0) == pl.num_programs(0) - 1)
+    def _():
+        copy_out.wait()
 
 
 def hidden_grad(at, scale, slots, weight, factor_pairs, first, width):
@@ -224,8 +230,12 @@
             + [pl.BlockSpec((2, 1, UNIT_STEP, depth), lambda i, at: (0, at[0], start + i, 0))]
             + [pl.BlockSpec((rows, UNIT_STEP), lambda i, at: (0, start + i))] * 8,
             out_specs=[pl.BlockSpec((2, rows, UNIT_STEP), lambda i, at: (0, 0, i))] * 4
-            + [pl.BlockSpec((2 * rows, depth), lambda i, at: (0, 0))],
-            scratch_shapes=[pltpu.VMEM((2, 2 * rows, UNIT_STEP), jnp.float32)],
+            + [pl.BlockSpec(memory_space=pl.ANY)],
+            scratch_shapes=[
+                pltpu.VMEM((2, 2 * rows, UNIT_STEP), jnp.float32),
+                pltpu.VMEM((2 * rows, depth), jnp.bfloat16),
+                pltpu.SemaphoreType.DMA,
+            ],
         ),
         out_shape=[out] * 4 + [jax.ShapeDtypeStruct((2 * rows, depth), jnp.bfloat16)],
         compiler_params=pltpu.CompilerParams(vmem_limit_bytes=VMEM_BYTES),

time: 98.8 us -> 98.3 us (level)
  no operation moved by 1% of the time
where the time goes in v4:
time: 98.3 us; the launch traced here: 97.9 us
  Pallas kernels  60.6 us (62%)
  starting transfers between devices  15 us (15%)
  waiting for transfers between devices  9.91 us (10%)
  local copies, waits for them, and re-layouts  9.36 us (10%)
  between operations  2.33 us (2%)
    pallas_call x1, Pallas kernels, hidden_grad(): pl.pallas_call(hidden_grad_kernel, grid_spec=pltpu.PrefetchScalarGridSpec...  21 us
    pallas_call x1, Pallas kernels, weight_grad(): pl.pallas_call(functools.partial(weight_grad_kernel, low_steps), grid_spe...  19.5 us
    pallas_call x4, Pallas kernels, factors(): pl.pallas_call(factors_kernel, grid_spec=pltpu.PrefetchScalarGridSpec(num...  13.8 us
    ppermute x6, starting transfers between devices, around(): lax.ppermute(value, 'tensor', [(i, (i + places) % 4) for i in range(4)])  7.17 us
    ppermute x13, waiting for transfers between devices, to_pair(): return lax.ppermute(value, 'dp', pair)  5.06 us
    ppermute x6, waiting for transfers between devices, around(): lax.ppermute(value, 'tensor', [(i, (i + places) % 4) for i in range(4)])  4.84 us
    ppermute x4, starting transfers between devices, to_across(): return lax.ppermute(value, 'dp', across)  4.62 us
    unnamed x40, local copies, waits for them, and re-layouts  4.19 us
  transfers between devices with their start and end apart: 23, of which 7 were waited for; matrix products, arithmetic and copies ran while one was open for 4% of the time, Pallas kernels for 62%

profile of v4, /device:TPU:0, one launch (start us, length us, event | category | flops | bytes accessed | tf_op | source)
XLA Modules:
  0.0 97.9 jit_solution(6772490169425945865)
XLA Ops:
  0.6 0.5 collective-permute-start.2
  1.1 2.6 %collective-permute-start = (bf16[48,4096]{1,0:T(8,128)(2,1)}, bf16[48,4096]{1,0:T(8,128)(2,1)S(1)}, u32[]{:S(2)}, u32[]{:S(2)}) collective-permute-start(bf16[48,4096]{1,0:T(8,128)(2,1)} %bitcast.39), channel_id=1, source_target_pairs={{0,4},{4,8},{8,12},{12,0},{1,5},{5,9},{9,13},{13,1},{2,6},{6,10},{... | collective-permute-start | bytes 1179656 | tf_op jit(solution)/shard_map/ppermute | solution.py:341
  3.8 1.0 %slice.24 = bf16[48,2560]{1,0:T(8,128)(2,1)S(1)} slice(bf16[48,4096]{1,0:T(8,128)(2,1)} %bitcast.40), slice={[0:48], [1536:4096]} | slice | bytes 491520 | tf_op jit(solution)/shard_map/slice | solution.py:346
  4.8 1.6 %collective-permute-start.1 = (bf16[48,2560]{1,0:T(8,128)(2,1)S(1)}, bf16[48,2560]{1,0:T(8,128)(2,1)}, u32[]{:S(2)}, u32[]{:S(2)}) collective-permute-start(bf16[48,2560]{1,0:T(8,128)(2,1)S(1)} %slice.24), channel_id=1, source_target_pairs={{0,2},{1,3},{2,0},{3,1},{4,6},{5,7},{6,4},{7,5},{8,10},{9,11},{10,... | collective-permute-start | bytes 737288 | tf_op jit(solution)/shard_map/ppermute | solution.py:338
  6.4 0.6 stack.31.at
  7.0 3.5 %factors.4 = (bf16[192,1792]{1,0:T(8,128)(2,1)}, bf16[192,1792]{1,0:T(8,128)(2,1)}, bf16[192,1792]{1,0:T(8,128)(2,1)}) custom-call(s32[7]{0:T(128)} %stack.31.at, bf16[192,7168]{1,0:T(8,128)(2,1)} %bitcast.32, bf16[192,7168]{1,0:T(8,128)(2,1)} %bitcast.35), custom_call_target="tpu_custom_call" | custom-call | flops 1000 | bytes 1000 | tf_op jit(solution)/shard_map/factors/pallas_call | solution.py:113
  10.5 3.6 %share.1 = (bf16[192,3584]{1,0:T(8,128)(2,1)}, bf16[192,3584]{1,0:T(8,128)(2,1)}) custom-call(s32[7]{0:T(128)} %stack.31.at, bf16[192,7168]{1,0:T(8,128)(2,1)} %bitcast.33, bf16[192,7168]{1,0:T(8,128)(2,1)} %bitcast.36), custom_call_target="tpu_custom_call" | custom-call | flops 1000 | bytes 1000 | tf_op jit(solution)/shard_map/share/pallas_call | solution.py:163
  14.1 1.6 %collective-permute-done.refs_1_ = bf16[48,4096]{1,0:T(8,128)(2,1)S(1)} collective-permute-done((bf16[48,4096]{1,0:T(8,128)(2,1)}, bf16[48,4096]{1,0:T(8,128)(2,1)S(1)}, u32[]{:S(2)}, u32[]{:S(2)}) %collective-permute-start) | collective-permute-done | bytes 393248 | tf_op jit(solution)/shard_map/ppermute | solution.py:341
  15.8 0.5 collective-permute-start.5
  16.3 0.1 collective-permute-start.6
  16.3 0.6 collective-permute-start.3
  17.0 0.9 collective-permute-start.10
  17.9 2.1 %collective-permute-done.6.refs_5_ = bf16[48,4096]{1,0:T(8,128)(2,1)S(1)} collective-permute-done((bf16[48,4096]{1,0:T(8,128)(2,1)S(1)}, bf16[48,4096]{1,0:T(8,128)(2,1)S(1)}, u32[]{:S(2)}, u32[]{:S(2)}) %collective-permute-start.6) | collective-permute-done | bytes 393248 | tf_op jit(solution)/shard_map/ppermute | solution.py:335
  20.0 0.7 copy-done.9
  20.8 0.9 collective-permute-done.5.up
  21.6 0.2 copy-done
  21.8 1.1 %copy-done.1 = bf16[192,3584]{1,0:T(8,128)(2,1)} copy-done((bf16[192,3584]{1,0:T(8,128)(2,1)}, bf16[192,3584]{1,0:T(8,128)(2,1)S(1)}, u32[]{:S(2)}) %copy-start.1) | copy-done | bytes 1376280
  22.9 3.5 %factors.5 = (bf16[192,1792]{1,0:T(8,128)(2,1)}, bf16[192,1792]{1,0:T(8,128)(2,1)}, bf16[192,1792]{1,0:T(8,128)(2,1)}) custom-call(s32[7]{0:T(128)} %stack.31.at, bf16[192,3584]{1,0:T(8,128)(2,1)} %copy-done, bf16[192,3584]{1,0:T(8,128)(2,1)} %copy-done.1), custom_call_target="tpu_custom_call" | custom-call | flops 1000 | bytes 1000 | tf_op jit(solution)/shard_map/factors/pallas_call | solution.py:113
  26.4 3.2 %collective-permute-done.3.refs_2_ = bf16[48,4096]{1,0:T(8,128)(2,1)S(1)} collective-permute-done((bf16[48,4096]{1,0:T(8,128)(2,1)S(1)}, bf16[48,4096]{1,0:T(8,128)(2,1)S(1)}, u32[]{:S(2)}, u32[]{:S(2)}) %collective-permute-start.3) | collective-permute-done | bytes 393248 | tf_op jit(solution)/shard_map/ppermute | solution.py:341
  29.6 0.5 collective-permute-start.9
  30.1 0.2 copy-done.3
  30.3 2.6 %assemble.1 = bf16[192,1536]{1,0:T(8,128)(2,1)} custom-call(s32[7]{0:T(128)} %stack.31.at, bf16[48,4096]{1,0:T(8,128)(2,1)} %bitcast.41, bf16[48,4096]{1,0:T(8,128)(2,1)} %copy-done.2, bf16[48,4096]{1,0:T(8,128)(2,1)} %copy-done.3), custom_call_target="tpu_custom_call" | custom-call | flops 1000 | bytes 1000 | tf_op jit(solution)/shard_map/assemble/pallas_call | solution.py:139
  32.9 3.4 %factors.7 = (bf16[192,1792]{1,0:T(8,128)(2,1)}, bf16[192,1792]{1,0:T(8,128)(2,1)}, bf16[192,1792]{1,0:T(8,128)(2,1)}) custom-call(s32[7]{0:T(128)} %stack.31.at, bf16[192,3584]{1,0:T(8,128)(2,1)} %copy-done, bf16[192,3584]{1,0:T(8,128)(2,1)} %copy-done.1), custom_call_target="tpu_custom_call" | custom-call | flops 1000 | bytes 1000 | tf_op jit(solution)/shard_map/factors/pallas_call | solution.py:113
  36.3 1.6 %collective-permute-start.12 = (bf16[192,1792]{1,0:T(8,128)(2,1)}, bf16[192,1792]{1,0:T(8,128)(2,1)S(1)}, u32[]{:S(2)}, u32[]{:S(2)}) collective-permute-start(bf16[192,1792]{1,0:T(8,128)(2,1)} %get-tuple-element.98), channel_id=1, source_target_pairs={{0,2},{1,3},{2,0},{3,1},{4,6},{5,7},{6,4},{7,5},{8,10},{9,11},{10,... | collective-permute-start | bytes 2064392 | tf_op jit(solution)/shard_map/ppermute | solution.py:338
  37.9 3.4 %factors.6 = (bf16[192,1792]{1,0:T(8,128)(2,1)}, bf16[192,1792]{1,0:T(8,128)(2,1)}, bf16[192,1792]{1,0:T(8,128)(2,1)}) custom-call(s32[7]{0:T(128)} %stack.31.at, bf16[192,7168]{1,0:T(8,128)(2,1)} %bitcast.34, bf16[192,7168]{1,0:T(8,128)(2,1)} %bitcast.37), custom_call_target="tpu_custom_call" | custom-call | flops 1000 | bytes 1000 | tf_op jit(solution)/shard_map/factors/pallas_call | solution.py:113
  41.4 0.7 fusion.5
  43.6 0.7 copy-done.12
  44.3 0.6 collective-permute-start.13
  44.9 3.3 %collective-permute-start.16 = (bf16[48,2560]{1,0:T(8,128)(2,1)}, bf16[48,2560]{1,0:T(8,128)(2,1)S(1)}, u32[]{:S(2)}, u32[]{:S(2)}) collective-permute-start(bf16[48,2560]{1,0:T(8,128)(2,1)} %collective-permute-done.1.refs_8_), channel_id=1, source_target_pairs={{0,12},{4,0},{8,4},{12,8},{1,13},{5,1},{9,5},{13,9},{2,14},{6,2},{... | collective-permute-start | bytes 737288 | tf_op jit(solution)/shard_map/ppermute | solution.py:341
  48.2 0.6 collective-permute-start.14
  48.8 0.2 copy-done.11
  49.0 21.0 %hidden_grad.1 = (bf16[2,192,1792]{2,1,0:T(8,128)(2,1)}, bf16[2,192,1792]{2,1,0:T(8,128)(2,1)}, bf16[2,192,1792]{2,1,0:T(8,128)(2,1)}, bf16[2,192,1792]{2,1,0:T(8,128)(2,1)}, bf16[384,4096]{1,0:T(8,128)(2,1)}) custom-call(s32[7]{0:T(128)} %stack.31.at, f32[1]{0:T(128)} %bitcast.10.scale, bf16[48,4096]{1,0:T(8,128)(2,1)} %bitcast.42, ...), custom_call_target="tpu_custom_call" | custom-call | flops 1000 | bytes 1000 | tf_op jit(solution)/shard_map/hidden_grad/pallas_call | solution.py:223
  70.1 0.1 collective-permute-start.17
  70.2 0.5 collective-permute-start.18
  70.7 0.1 collective-permute-start.19
  70.8 0.4 collective-permute-start.20
  71.2 1.3 %collective-permute-done.18.refs_13_ = bf16[48,2560]{1,0:T(8,128)(2,1)S(1)} collective-permute-done((bf16[48,2560]{1,0:T(8,128)(2,1)S(1)}, bf16[48,2560]{1,0:T(8,128)(2,1)S(1)}, u32[]{:S(2)}, u32[]{:S(2)}) %collective-permute-start.18) | collective-permute-done | bytes 245792 | tf_op jit(solution)/shard_map/ppermute | solution.py:335
  72.5 0.3 collective-permute-done.19.refs_14_
  72.9 0.3 collective-permute-done.20.refs_15_
  73.2 0.3 copy-done.17
  73.6 0.7 copy-done.18
  74.2 0.2 collective-permute-start.21
  74.5 0.4 collective-permute-start.22
  74.8 19.5 %weight_grad.1 = (bf16[192,7168]{1,0:T(8,128)(2,1)}, bf16[192,7168]{1,0:T(8,128)(2,1)}, bf16[1792,4096]{1,0:T(8,128)(2,1)}) custom-call(s32[7]{0:T(128)} %stack.31.at, f32[1]{0:T(128)S(6)} %div.18.norm, bf16[192,1792]{1,0:T(8,128)(2,1)} %get-tuple-element.78.refs_0_, bf16[192,1792]{1,0:T(8,128)(2,1)} %get-tuple-element.80.refs_1_, ...), custom_call_target="tpu_custom_call" | custom-call | flops 1000 | bytes 1000 | tf_op jit(solution)/shard_map/weight_grad/pallas_call | solution.py:301
  94.3 0.9 fusion.3
  95.2 0.9 fusion.2
  96.1 0.9 fusion.1
  97.0 0.9 fusion
  (54 shorter events, 0.1 us)
Async XLA Ops:
  0.6 13.5 %collective-permute-start.2 = (bf16[48,4096]{1,0:T(8,128)(2,1)}, bf16[48,4096]{1,0:T(8,128)(2,1)S(1)}, u32[]{:S(2)}, u32[]{:S(2)}) collective-permute-start(bf16[48,4096]{1,0:T(8,128)(2,1)} %bitcast.38), channel_id=1, source_target_pairs={{0,1},{1,0},{2,3},{3,2},{4,5},{5,4},{6,7},{7,6},{8,9},{9,8},{10,11... | collective-permute-start | bytes 1179656 | tf_op jit(solution)/shard_map/ppermute | solution.py:335
  1.1 14.6 %collective-permute-start = (bf16[48,4096]{1,0:T(8,128)(2,1)}, bf16[48,4096]{1,0:T(8,128)(2,1)S(1)}, u32[]{:S(2)}, u32[]{:S(2)}) collective-permute-start(bf16[48,4096]{1,0:T(8,128)(2,1)} %bitcast.39), channel_id=1, source_target_pairs={{0,4},{4,8},{8,12},{12,0},{1,5},{5,9},{9,13},{13,1},{2,6},{6,10},{... | collective-permute-start | bytes 1179656 | tf_op jit(solution)/shard_map/ppermute | solution.py:341
  4.8 9.3 %collective-permute-start.1 = (bf16[48,2560]{1,0:T(8,128)(2,1)S(1)}, bf16[48,2560]{1,0:T(8,128)(2,1)}, u32[]{:S(2)}, u32[]{:S(2)}) collective-permute-start(bf16[48,2560]{1,0:T(8,128)(2,1)S(1)} %slice.24), channel_id=1, source_target_pairs={{0,2},{1,3},{2,0},{3,1},{4,6},{5,7},{6,4},{7,5},{8,10},{9,11},{10,... | collective-permute-start | bytes 737288 | tf_op jit(solution)/shard_map/ppermute | solution.py:338
  14.1 1.6 %copy-start.8 = (bf16[48,4096]{1,0:T(8,128)(2,1)}, bf16[48,4096]{1,0:T(8,128)(2,1)S(1)}, u32[]{:S(2)}) copy-start(bf16[48,4096]{1,0:T(8,128)(2,1)S(1)} %collective-permute-done.2.refs_4_) | copy-start | bytes 1179652
  15.7 14.4 %copy-start.2 = (bf16[48,4096]{1,0:T(8,128)(2,1)}, bf16[48,4096]{1,0:T(8,128)(2,1)S(1)}, u32[]{:S(2)}) copy-start(bf16[48,4096]{1,0:T(8,128)(2,1)S(1)} %collective-permute-done.refs_1_) | copy-start | bytes 1179652
  15.7 4.3 %collective-permute-start.4 = (bf16[192,3584]{1,0:T(8,128)(2,1)}, bf16[192,3584]{1,0:T(8,128)(2,1)S(1)}, u32[]{:S(2)}, u32[]{:S(2)}) collective-permute-start(bf16[192,3584]{1,0:T(8,128)(2,1)} %get-tuple-element.67), channel_id=1, source_target_pairs={{0,1},{1,0},{2,3},{3,2},{4,5},{5,4},{6,7},{7,6},{8,9},{9,8},{10,11... | collective-permute-start | bytes 4128776 | tf_op jit(solution)/shard_map/ppermute | solution.py:335
  15.8 5.9 %collective-permute-start.5 = (bf16[192,3584]{1,0:T(8,128)(2,1)}, bf16[192,3584]{1,0:T(8,128)(2,1)S(1)}, u32[]{:S(2)}, u32[]{:S(2)}) collective-permute-start(bf16[192,3584]{1,0:T(8,128)(2,1)} %get-tuple-element.68), channel_id=1, source_target_pairs={{0,1},{1,0},{2,3},{3,2},{4,5},{5,4},{6,7},{7,6},{8,9},{9,8},{10,11... | collective-permute-start | bytes 4128776 | tf_op jit(solution)/shard_map/ppermute | solution.py:335
  16.3 3.7 %collective-permute-start.6 = (bf16[48,4096]{1,0:T(8,128)(2,1)S(1)}, bf16[48,4096]{1,0:T(8,128)(2,1)S(1)}, u32[]{:S(2)}, u32[]{:S(2)}) collective-permute-start(bf16[48,4096]{1,0:T(8,128)(2,1)S(1)} %collective-permute-done.refs_1_), channel_id=1, source_target_pairs={{0,1},{1,0},{2,3},{3,2},{4,5},{5,4},{6,7},{7,6},{8,9},{9,8},{10,11... | collective-permute-start | bytes 1179656 | tf_op jit(solution)/shard_map/ppermute | solution.py:335
  16.3 13.3 %collective-permute-start.3 = (bf16[48,4096]{1,0:T(8,128)(2,1)S(1)}, bf16[48,4096]{1,0:T(8,128)(2,1)S(1)}, u32[]{:S(2)}, u32[]{:S(2)}) collective-permute-start(bf16[48,4096]{1,0:T(8,128)(2,1)S(1)} %collective-permute-done.refs_1_), channel_id=1, source_target_pairs={{0,4},{4,8},{8,12},{12,0},{1,5},{5,9},{9,13},{13,1},{2,6},{6,10},{... | collective-permute-start | bytes 1179656 | tf_op jit(solution)/shard_map/ppermute | solution.py:341
  17.0 26.6 %collective-permute-start.10 = (bf16[192,1792]{1,0:T(8,128)(2,1)}, bf16[192,1792]{1,0:T(8,128)(2,1)}, u32[]{:S(2)}, u32[]{:S(2)}) collective-permute-start(bf16[192,1792]{1,0:T(8,128)(2,1)} %get-tuple-element.75), channel_id=1, source_target_pairs={{0,2},{1,3},{2,0},{3,1},{4,6},{5,7},{6,4},{7,5},{8,10},{9,11},{10,... | collective-permute-start | bytes 2064392 | tf_op jit(solution)/shard_map/ppermute | solution.py:338
  20.0 0.8 copy-start.9
  20.8 1.1 %copy-start = (bf16[192,3584]{1,0:T(8,128)(2,1)}, bf16[192,3584]{1,0:T(8,128)(2,1)S(1)}, u32[]{:S(2)}) copy-start(bf16[192,3584]{1,0:T(8,128)(2,1)S(1)} %collective-permute-done.4.gate) | copy-start | bytes 4128772
  21.8 1.1 %copy-start.1 = (bf16[192,3584]{1,0:T(8,128)(2,1)}, bf16[192,3584]{1,0:T(8,128)(2,1)S(1)}, u32[]{:S(2)}) copy-start(bf16[192,3584]{1,0:T(8,128)(2,1)S(1)} %collective-permute-done.5.up) | copy-start | bytes 4128772
  29.6 0.7 copy-start.3
  29.6 14.0 %collective-permute-start.8 = (bf16[48,4096]{1,0:T(8,128)(2,1)S(1)}, bf16[48,4096]{1,0:T(8,128)(2,1)S(1)}, u32[]{:S(2)}, u32[]{:S(2)}) collective-permute-start(bf16[48,4096]{1,0:T(8,128)(2,1)S(1)} %collective-permute-done.3.refs_2_), channel_id=1, source_target_pairs={{0,1},{1,0},{2,3},{3,2},{4,5},{5,4},{6,7},{7,6},{8,9},{9,8},{10,11... | collective-permute-start | bytes 1179656 | tf_op jit(solution)/shard_map/ppermute | solution.py:335
  29.6 14.0 %collective-permute-start.7 = (bf16[48,4096]{1,0:T(8,128)(2,1)S(1)}, bf16[48,4096]{1,0:T(8,128)(2,1)S(1)}, u32[]{:S(2)}, u32[]{:S(2)}) collective-permute-start(bf16[48,4096]{1,0:T(8,128)(2,1)S(1)} %collective-permute-done.3.refs_2_), channel_id=1, source_target_pairs={{0,4},{4,8},{8,12},{12,0},{1,5},{5,9},{9,13},{13,1},{2,6},{6,10},{... | collective-permute-start | bytes 1179656 | tf_op jit(solution)/shard_map/ppermute | solution.py:341
  29.6 14.0 %collective-permute-start.9 = (bf16[48,2560]{1,0:T(8,128)(2,1)}, bf16[48,2560]{1,0:T(8,128)(2,1)S(1)}, u32[]{:S(2)}, u32[]{:S(2)}) collective-permute-start(bf16[48,2560]{1,0:T(8,128)(2,1)} %collective-permute-done.1.refs_8_), channel_id=1, source_target_pairs={{0,1},{1,0},{2,3},{3,2},{4,5},{5,4},{6,7},{7,6},{8,9},{9,8},{10,11... | collective-permute-start | bytes 737288 | tf_op jit(solution)/shard_map/ppermute | solution.py:335
  36.3 5.0 %copy-start.19 = (s32[2]{0:T(128)S(1)}, s32[2]{0:T(128)}, u32[]{:S(2)}) copy-start(s32[2]{0:T(128)} %param.5) | copy-start | bytes 28
  36.3 7.9 %copy-start.6 = (bf16[192,1536]{1,0:T(8,128)(2,1)S(1)}, bf16[192,1536]{1,0:T(8,128)(2,1)}, u32[]{:S(2)}) copy-start(bf16[192,1536]{1,0:T(8,128)(2,1)} %assemble.1) | copy-start | bytes 1769476
  36.3 33.7 %collective-permute-start.12 = (bf16[192,1792]{1,0:T(8,128)(2,1)}, bf16[192,1792]{1,0:T(8,128)(2,1)S(1)}, u32[]{:S(2)}, u32[]{:S(2)}) collective-permute-start(bf16[192,1792]{1,0:T(8,128)(2,1)} %get-tuple-element.98), channel_id=1, source_target_pairs={{0,2},{1,3},{2,0},{3,1},{4,6},{5,7},{6,4},{7,5},{8,10},{9,11},{10,... | collective-permute-start | bytes 2064392 | tf_op jit(solution)/shard_map/ppermute | solution.py:338
  43.6 0.7 copy-start.12
  43.6 5.2 %copy-start.10 = (bf16[48,4096]{1,0:T(8,128)(2,1)}, bf16[48,4096]{1,0:T(8,128)(2,1)S(1)}, u32[]{:S(2)}) copy-start(bf16[48,4096]{1,0:T(8,128)(2,1)S(1)} %collective-permute-done.8.refs_6_) | copy-start | bytes 1179652
  43.6 5.2 %copy-start.4 = (bf16[48,4096]{1,0:T(8,128)(2,1)}, bf16[48,4096]{1,0:T(8,128)(2,1)S(1)}, u32[]{:S(2)}) copy-start(bf16[48,4096]{1,0:T(8,128)(2,1)S(1)} %collective-permute-done.7.refs_3_) | copy-start | bytes 1179652
  44.3 3.9 %collective-permute-start.11 = (bf16[48,4096]{1,0:T(8,128)(2,1)S(1)}, bf16[48,4096]{1,0:T(8,128)(2,1)S(1)}, u32[]{:S(2)}, u32[]{:S(2)}) collective-permute-start(bf16[48,4096]{1,0:T(8,128)(2,1)S(1)} %collective-permute-done.7.refs_3_), channel_id=1, source_target_pairs={{0,1},{1,0},{2,3},{3,2},{4,5},{5,4},{6,7},{7,6},{8,9},{9,8},{10,11... | collective-permute-start | bytes 1179656 | tf_op jit(solution)/shard_map/ppermute | solution.py:335
  44.3 25.8 %collective-permute-start.13 = (bf16[192,1536]{1,0:T(8,128)(2,1)S(1)}, bf16[192,1536]{1,0:T(8,128)(2,1)S(1)}, u32[]{:S(2)}, u32[]{:S(2)}) collective-permute-start(bf16[192,1536]{1,0:T(8,128)(2,1)S(1)} %slice_dynamic-update-slice_fusion), channel_id=1, source_target_pairs={{0,2},{1,3},{2,0},{3,1},{4,6},{5,7},{6,4},{7,5},{8,10},{9,11},{10,... | collective-permute-start | bytes 1769480 | tf_op jit(solution)/shard_map/ppermute | solution.py:338
  44.9 25.1 %collective-permute-start.16 = (bf16[48,2560]{1,0:T(8,128)(2,1)}, bf16[48,2560]{1,0:T(8,128)(2,1)S(1)}, u32[]{:S(2)}, u32[]{:S(2)}) collective-permute-start(bf16[48,2560]{1,0:T(8,128)(2,1)} %collective-permute-done.1.refs_8_), channel_id=1, source_target_pairs={{0,12},{4,0},{8,4},{12,8},{1,13},{5,1},{9,5},{13,9},{2,14},{6,2},{... | collective-permute-start | bytes 737288 | tf_op jit(solution)/shard_map/ppermute | solution.py:341
  48.2 21.8 %collective-permute-start.15 = (bf16[48,2560]{1,0:T(8,128)(2,1)}, bf16[48,2560]{1,0:T(8,128)(2,1)S(1)}, u32[]{:S(2)}, u32[]{:S(2)}) collective-permute-start(bf16[48,2560]{1,0:T(8,128)(2,1)} %collective-permute-done.1.refs_8_), channel_id=1, source_target_pairs={{0,8},{4,12},{8,0},{12,4},{1,9},{5,13},{9,1},{13,5},{2,10},{6,14},... | collective-permute-start | bytes 737288 | tf_op jit(solution)/shard_map/ppermute | solution.py:341
  48.2 0.8 copy-start.11
  48.2 21.8 %collective-permute-start.14 = (bf16[48,2560]{1,0:T(8,128)(2,1)}, bf16[48,2560]{1,0:T(8,128)(2,1)S(1)}, u32[]{:S(2)}, u32[]{:S(2)}) collective-permute-start(bf16[48,2560]{1,0:T(8,128)(2,1)} %collective-permute-done.1.refs_8_), channel_id=1, source_target_pairs={{0,4},{4,8},{8,12},{12,0},{1,5},{5,9},{9,13},{13,1},{2,6},{6,10},{... | collective-permute-start | bytes 737288 | tf_op jit(solution)/shard_map/ppermute | solution.py:341
  70.0 3.2 %copy-start.13 = (bf16[48,2560]{1,0:T(8,128)(2,1)}, bf16[48,2560]{1,0:T(8,128)(2,1)S(1)}, u32[]{:S(2)}) copy-start(bf16[48,2560]{1,0:T(8,128)(2,1)S(1)} %collective-permute-done.16.refs_11_) | copy-start | bytes 737284
  70.0 4.4 %copy-start.14 = (bf16[48,2560]{1,0:T(8,128)(2,1)}, bf16[48,2560]{1,0:T(8,128)(2,1)S(1)}, u32[]{:S(2)}) copy-start(bf16[48,2560]{1,0:T(8,128)(2,1)S(1)} %collective-permute-done.15.refs_10_) | copy-start | bytes 737284
  70.0 4.4 %copy-start.15 = (bf16[48,2560]{1,0:T(8,128)(2,1)}, bf16[48,2560]{1,0:T(8,128)(2,1)S(1)}, u32[]{:S(2)}) copy-start(bf16[48,2560]{1,0:T(8,128)(2,1)S(1)} %collective-permute-done.14.refs_9_) | copy-start | bytes 737284
  70.1 4.2 %copy-start.5 = (bf16[192,1792]{1,0:T(8,128)(2,1)}, bf16[192,1792]{1,0:T(8,128)(2,1)S(1)}, u32[]{:S(2)}) copy-start(bf16[192,1792]{1,0:T(8,128)(2,1)S(1)} %collective-permute-done.12.refs_3_) | copy-start | bytes 2064388
  70.1 4.7 %copy-start.7 = (bf16[192,1536]{1,0:T(8,128)(2,1)}, bf16[192,1536]{1,0:T(8,128)(2,1)S(1)}, u32[]{:S(2)}) copy-start(bf16[192,1536]{1,0:T(8,128)(2,1)S(1)} %collective-permute-done.13.refs_6_) | copy-start | bytes 1769476
  70.1 4.1 %collective-permute-start.17 = (bf16[192,1536]{1,0:T(8,128)(2,1)S(1)}, bf16[192,1536]{1,0:T(8,128)(2,1)}, u32[]{:S(2)}, u32[]{:S(2)}) collective-permute-start(bf16[192,1536]{1,0:T(8,128)(2,1)S(1)} %collective-permute-done.13.refs_6_), channel_id=1, source_target_pairs={{0,1},{1,0},{2,3},{3,2},{4,5},{5,4},{6,7},{7,6},{8,9},{9,8},{10,11... | collective-permute-start | bytes 1769480 | tf_op jit(solution)/shard_map/ppermute | solution.py:335
  70.2 2.3 %collective-permute-start.18 = (bf16[48,2560]{1,0:T(8,128)(2,1)S(1)}, bf16[48,2560]{1,0:T(8,128)(2,1)S(1)}, u32[]{:S(2)}, u32[]{:S(2)}) collective-permute-start(bf16[48,2560]{1,0:T(8,128)(2,1)S(1)} %collective-permute-done.14.refs_9_), channel_id=1, source_target_pairs={{0,1},{1,0},{2,3},{3,2},{4,5},{5,4},{6,7},{7,6},{8,9},{9,8},{10,11... | collective-permute-start | bytes 737288 | tf_op jit(solution)/shard_map/ppermute | solution.py:335
  70.7 2.2 %collective-permute-start.19 = (bf16[48,2560]{1,0:T(8,128)(2,1)S(1)}, bf16[48,2560]{1,0:T(8,128)(2,1)S(1)}, u32[]{:S(2)}, u32[]{:S(2)}) collective-permute-start(bf16[48,2560]{1,0:T(8,128)(2,1)S(1)} %collective-permute-done.15.refs_10_), channel_id=1, source_target_pairs={{0,1},{1,0},{2,3},{3,2},{4,5},{5,4},{6,7},{7,6},{8,9},{9,8},{10,11... | collective-permute-start | bytes 737288 | tf_op jit(solution)/shard_map/ppermute | solution.py:335
  70.8 2.5 %collective-permute-start.20 = (bf16[48,2560]{1,0:T(8,128)(2,1)S(1)}, bf16[48,2560]{1,0:T(8,128)(2,1)S(1)}, u32[]{:S(2)}, u32[]{:S(2)}) collective-permute-start(bf16[48,2560]{1,0:T(8,128)(2,1)S(1)} %collective-permute-done.16.refs_11_), channel_id=1, source_target_pairs={{0,1},{1,0},{2,3},{3,2},{4,5},{5,4},{6,7},{7,6},{8,9},{9,8},{10,11... | collective-permute-start | bytes 737288 | tf_op jit(solution)/shard_map/ppermute | solution.py:335
  72.5 1.7 %copy-start.16 = (bf16[48,2560]{1,0:T(8,128)(2,1)}, bf16[48,2560]{1,0:T(8,128)(2,1)S(1)}, u32[]{:S(2)}) copy-start(bf16[48,2560]{1,0:T(8,128)(2,1)S(1)} %collective-permute-done.18.refs_13_) | copy-start | bytes 737284
  72.9 0.7 copy-start.17
  73.6 0.7 copy-start.18
  74.2 20.1 %collective-permute-start.21 = (bf16[2,192,1792]{2,1,0:T(8,128)(2,1)}, bf16[2,192,1792]{2,1,0:T(8,128)(2,1)S(1)}, u32[]{:S(2)}, u32[]{:S(2)}) collective-permute-start(bf16[2,192,1792]{2,1,0:T(8,128)(2,1)} %get-tuple-element.119), channel_id=1, source_target_pairs={{0,1},{1,0},{2,3},{3,2},{4,5},{5,4},{6,7},{7,6},{8,9},{9,8},{10,11... | collective-permute-start | bytes 4128776 | tf_op jit(solution)/shard_map/ppermute | solution.py:335
  74.5 21.7 %collective-permute-start.22 = (bf16[2,192,1792]{2,1,0:T(8,128)(2,1)}, bf16[2,192,1792]{2,1,0:T(8,128)(2,1)S(1)}, u32[]{:S(2)}, u32[]{:S(2)}) collective-permute-start(bf16[2,192,1792]{2,1,0:T(8,128)(2,1)} %get-tuple-element.121), channel_id=1, source_target_pairs={{0,1},{1,0},{2,3},{3,2},{4,5},{5,4},{6,7},{7,6},{8,9},{9,8},{10,11... | collective-permute-start | bytes 4128776 | tf_op jit(solution)/shard_map/ppermute | solution.py:335
